TPU v7x, 512 devices: a whole 4x8x8 slice. The times are simulated.
512 devices in a mesh: seq: 128 (over z, x, y_lo), head: 4 (over y_hi, core).
Axes of the slice: x: 4, y: 8 (y_hi: 2, y_lo: 4; y = y_hi * 4 + y_lo), z: 8, core: 2. Of those that a mesh axis runs over, the one named last changes fastest.
Arguments:
- query_rows: bfloat16 [32768, 1536], P('seq', 'head'), may hold values from -6 to 6
- key_rows: bfloat16 [32768, 1536], P('seq', 'head'), may hold values from -6 to 6
- value_rows: bfloat16 [32768, 1536], P('seq', 'head'), may hold values from -4 to 4
- out_weight: bfloat16 [1536, 1536], P(None, 'head'), may hold values from -0.15625 to 0.15625
- out_grad: bfloat16 [32768, 1536], P('seq', 'head'), may hold values from -24 to 24
Outputs:
- projected: bfloat16 [32768, 1536], P('seq', 'head')
- query_grad: bfloat16 [32768, 1536], P('seq', 'head')
- key_grad: bfloat16 [32768, 1536], P('seq', 'head')
- value_grad: bfloat16 [32768, 1536], P('seq', 'head')
- weight_grad: float32 [1536, 1536], P('seq', 'head')
All inputs are finite; a program needn't handle non-finite values.
Results may differ from a plain program's by a relative error of at most 0.035.
Values may be sent and summed in bfloat16 or wider, within the bound.
A program may use at most 64 MiB of HBM per device.

v0:
```python
import jax
import jax.numpy as jnp
from jax import lax
from jax.sharding import PartitionSpec as P

D = 1536
HEADS = 24
LOOKBACK = 4


def shifted(block, axis, distance):
    devices = range(lax.axis_size(axis))
    route = [(i - distance, i) for i in devices if i - distance in devices]
    return lax.ppermute(block, axis, route)


def window_probs(query_grp, key_grp, key_valid, score_scale):
    scores = (
        jnp.einsum("qhe,khe->hqk", query_grp, key_grp, preferred_element_type=jnp.float32)
        * score_scale
    )
    scores = jnp.where(key_valid[None, None, :], scores, -jnp.inf)
    row_max = jnp.max(scores, axis=-1, keepdims=True)
    exp_scores = jnp.exp(scores - row_max)
    return exp_scores / jnp.sum(exp_scores, axis=-1, keepdims=True)


def shards(query_rows, key_rows, value_rows, out_weight, out_grad):
    span_len = query_rows.shape[0]
    width_local = query_rows.shape[1]
    heads_local = HEADS // lax.axis_size("head")
    head_width = width_local // heads_local
    score_scale = float(head_width) ** (-0.5)
    window = (LOOKBACK + 1) * span_len
    position = lax.axis_index("seq")
    earlier = []
    for offset in range(LOOKBACK, 0, -1):
        earlier.append(shifted((key_rows, value_rows), "seq", offset))
    key_window = jnp.concatenate([member[0] for member in earlier] + [key_rows], axis=0)
    value_window = jnp.concatenate([member[1] for member in earlier] + [value_rows], axis=0)
    block_of = jnp.arange(window, dtype=jnp.int32) // span_len
    key_valid = position - LOOKBACK + block_of >= 0
    per_group = 2
    groups = heads_local // per_group
    group_cols = per_group * head_width

    def group_inputs(group_idx):
        first_col = group_idx * group_cols
        query_grp = query_rows[:, first_col : first_col + group_cols].reshape(
            span_len, per_group, head_width
        )
        key_grp = key_window[:, first_col : first_col + group_cols].reshape(
            window, per_group, head_width
        )
        value_grp = value_window[:, first_col : first_col + group_cols].reshape(
            window, per_group, head_width
        )
        return (query_grp, key_grp, value_grp)

    pieces = []
    kept_probs = []
    for group_idx in range(groups):
        query_grp, key_grp, value_grp = group_inputs(group_idx)
        attn_probs = window_probs(query_grp, key_grp, key_valid, score_scale)
        kept_probs.append(attn_probs)
        probs_low = attn_probs.astype(jnp.bfloat16)
        pieces.append(
            jnp.einsum(
                "hqk,khe->qhe", probs_low, value_grp, preferred_element_type=jnp.float32
            ).reshape(span_len, group_cols)
        )
    attended = jnp.concatenate(pieces, axis=1).astype(jnp.bfloat16)
    partial_value = lax.dot_general(
        attended, out_weight, (((1,), (1,)), ((), ())), preferred_element_type=jnp.float32
    )
    summed_all = lax.psum(partial_value, "head")
    out_width = D // lax.axis_size("head")
    projected = lax.dynamic_slice_in_dim(
        summed_all, lax.axis_index("head") * out_width, out_width, 1
    )
    projected = projected.astype(jnp.bfloat16)
    grad_full = lax.all_gather(out_grad, "head", axis=1, tiled=True)
    d_attended = jnp.dot(grad_full, out_weight, preferred_element_type=jnp.float32).astype(
        jnp.bfloat16
    )
    query_pieces = []
    key_pieces = []
    value_pieces = []
    for group_idx in range(groups):
        query_grp, key_grp, value_grp = group_inputs(group_idx)
        first_col = group_idx * group_cols
        dout_grp = d_attended[:, first_col : first_col + group_cols].reshape(
            span_len, per_group, head_width
        )
        attn_grp = attended[:, first_col : first_col + group_cols].reshape(
            span_len, per_group, head_width
        )
        attn_probs = kept_probs[group_idx]
        probs_low = attn_probs.astype(jnp.bfloat16)
        row_delta = jnp.einsum(
            "qhe,qhe->hq", dout_grp.astype(jnp.float32), attn_grp.astype(jnp.float32)
        )
        d_probs = jnp.einsum(
            "qhe,khe->hqk", dout_grp, value_grp, preferred_element_type=jnp.float32
        )
        d_scores = (attn_probs * (d_probs - row_delta[:, :, None])).astype(jnp.bfloat16)
        query_pieces.append(
            (
                jnp.einsum("hqk,khe->qhe", d_scores, key_grp, preferred_element_type=jnp.float32)
                * score_scale
            ).reshape(span_len, group_cols)
        )
        key_pieces.append(
            (
                jnp.einsum("hqk,qhe->khe", d_scores, query_grp, preferred_element_type=jnp.float32)
                * score_scale
            ).reshape(window, group_cols)
        )
        value_pieces.append(
            jnp.einsum(
                "hqk,qhe->khe", probs_low, dout_grp, preferred_element_type=jnp.float32
            ).reshape(window, group_cols)
        )
    query_grad = jnp.concatenate(query_pieces, axis=1).astype(jnp.bfloat16)
    key_terms = jnp.concatenate(key_pieces, axis=1)
    value_terms = jnp.concatenate(value_pieces, axis=1)
    own_start = LOOKBACK * span_len
    key_total = key_terms[own_start:]
    value_total = value_terms[own_start:]
    for offset in range(1, LOOKBACK + 1):
        first_row = (LOOKBACK - offset) * span_len
        arrived = shifted(
            (
                key_terms[first_row : first_row + span_len],
                value_terms[first_row : first_row + span_len],
            ),
            "seq",
            -offset,
        )
        key_total = key_total + arrived[0]
        value_total = value_total + arrived[1]
    weight_grad = lax.psum_scatter(
        lax.dot_general(
            grad_full, attended, (((0,), (0,)), ((), ())), preferred_element_type=jnp.float32
        ),
        "seq",
        scatter_dimension=0,
        tiled=True,
    )
    return (
        projected,
        query_grad,
        key_total.astype(jnp.bfloat16),
        value_total.astype(jnp.bfloat16),
        weight_grad,
    )


def solution(mesh):
    in_specs = (
        P("seq", "head"),
        P("seq", "head"),
        P("seq", "head"),
        P(None, "head"),
        P("seq", "head"),
    )
    out_specs = (
        P("seq", "head"),
        P("seq", "head"),
        P("seq", "head"),
        P("seq", "head"),
        P("seq", "head"),
    )
    return jax.shard_map(shards, mesh=mesh, in_specs=in_specs, out_specs=out_specs, check_vma=False)
```

profile of v0, /device:TPU:8, one launch (start us, length us, event | category | flops | bytes accessed | tf_op | source)
XLA Modules:
  0.0 1561.0 jit_solution(12048683109731580914)
XLA Ops:
  7.2 4.6 collective-permute-start.6
  11.9 4.0 collective-permute-start.5
  15.8 3.4 collective-permute-start.4
  19.2 3.2 collective-permute-start.1
  22.5 4.9 collective-permute-start
  27.3 0.9 fusion.60
  28.3 16.4 %all_gather.3 = bf16[256,1536]{1,0:T(8,128)(2,1)S(1)} all-gather(bf16[256,384]{1,0:T(8,128)(2,1)} %param.9), channel_id=1, replica_groups=mesh['seq'=128,'head'=4] {'head'}, dimensions={1}, use_global_device_ids=true | all-gather | bytes 983040 | tf_op jit(solution)/shard_map/all_gather | solution.py:82
  47.3 1.3 dynamic-slice
  49.2 1.3 collective-permute-start.2
  50.5 0.9 constant_dynamic-update-slice_fusion.4
  51.5 5.8 collective-permute-start.3
  57.3 2.7 collective-permute-done.2
  60.1 9.3 collective-permute-start.7
  69.5 1.0 fusion.58
  70.8 0.9 constant_dynamic-update-slice_fusion.9
  71.7 1.0 constant_dynamic-update-slice_fusion.8
  72.7 1.0 collective-permute-done.7
  73.7 1.0 constant_dynamic-update-slice_fusion.6
  74.7 1.0 fusion.57
  75.9 2.4 fusion.62
  78.4 2.0 fusion.25
  81.2 0.8 copy-done.2
  82.7 1.0 fusion.22
  84.2 1.9 copy.95
  86.1 1.9 copy.96
  87.9 3.4 fusion.61
  91.4 2.0 fusion.26
  93.8 1.4 fusion.66
  96.1 1.0 fusion.23
  97.1 1.4 convolution_multiply_fusion.3
  98.5 1.9 copy.87
  100.3 1.9 copy.88
  102.2 3.4 fusion.63
  105.6 2.0 fusion.24
  108.0 1.4 fusion.64
  110.7 1.4 convolution_multiply_fusion.5
  112.1 1.9 convolution_bitcast_fusion
  114.0 1.8 fusion.38
  115.8 1.1 copy.121
  116.9 1.1 copy.115
  118.7 1.1 copy.122
  119.8 1.1 copy.116
  121.6 1.2 copy.120
  122.8 1.1 copy.114
  124.6 1.6 pad_maximum_fusion
  126.3 1.0 fusion.56
  127.3 1.9 collective-permute-start.8
  129.2 1.3 collective-permute-start.11
  130.5 1.3 collective-permute-start.10
  131.8 1.3 collective-permute-start.9
  133.1 52.2 %all-reduce.5 = bf16[256,1536]{1,0:T(8,128)(2,1)} all-reduce(f32[256,1536]{1,0:T(8,128)} %fusion.38), channel_id=1, replica_groups=mesh['seq'=128,'head'=4] {'head'}, use_global_device_ids=true, to_apply=%region_6.7 | all-reduce | flops 393216 | bytes 2359296 | tf_op jit(solution)/shard_map/psum | solution.py:76
  185.3 1.6 pad_maximum_fusion.1
  187.0 1.9 collective-permute-start.12
  189.0 1.6 dynamic-slice_convert_fusion
  190.6 1.3 collective-permute-start.15
  191.9 1.3 collective-permute-start.14
  193.2 1.3 collective-permute-start.13
  195.2 2.1 fusion.34
  197.4 33.7 %collective-permute-done.12 = f32[256,384]{1,0:T(8,128)S(1)} collective-permute-done((f32[256,384]{1,0:T(8,128)S(1)}, f32[256,384]{1,0:T(8,128)S(1)}, u32[]{:S(2)}, u32[]{:S(2)}) %collective-permute-start.12) | collective-permute-done | bytes 393248 | tf_op jit(solution)/shard_map/ppermute | solution.py:14
  231.1 12.3 collective-permute-done.15
  243.4 9.1 collective-permute-done.14
  252.5 6.6 collective-permute-done.13
  259.9 1292.4 %all-reduce.4.cloned.1.call-done = f32[1536,384]{0,1:T(8,128)} async-done(((f32[1536,384]{0,1:T(8,128)}), f32[1536,384]{0,1:T(8,128)}) %all-reduce.4.cloned.1.call-update) | async-done | bytes 2359312
  1552.3 1.1 constant_dynamic-slice_fusion
  (94 shorter events, 12.8 us)
Async XLA Ops:
  7.2 37.5 %copy-start = (bf16[1536,384]{1,0:T(8,128)(2,1)S(1)}, bf16[1536,384]{1,0:T(8,128)(2,1)}, u32[]{:S(2)}) copy-start(bf16[1536,384]{1,0:T(8,128)(2,1)} %param.8) | copy-start | bytes 3538948
  7.2 1545.1 %all-reduce.4.cloned.1.call-start = ((), (), s32[]{:S(2)}) async-start(), calls=%async_computation | async-start | bytes 4718592
  7.2 65.5 %collective-permute-start.6 = (bf16[256,384]{1,0:T(8,128)(2,1)}, bf16[256,384]{1,0:T(8,128)(2,1)S(1)}, u32[]{:S(2)}, u32[]{:S(2)}) collective-permute-start(bf16[256,384]{1,0:T(8,128)(2,1)} %param.6), channel_id=1, source_target_pairs={{0,8},{4,12},{8,16},{12,20},{16,24},{20,28},{24,32},{28,36},{32,40... | collective-permute-start | bytes 589832 | tf_op jit(solution)/shard_map/ppermute | solution.py:14
  11.9 59.8 %collective-permute-start.5 = (bf16[256,384]{1,0:T(8,128)(2,1)}, bf16[256,384]{1,0:T(8,128)(2,1)}, u32[]{:S(2)}, u32[]{:S(2)}) collective-permute-start(bf16[256,384]{1,0:T(8,128)(2,1)} %param.6), channel_id=1, source_target_pairs={{0,12},{4,16},{8,20},{12,24},{16,28},{20,32},{24,36},{28,40},{32,4... | collective-permute-start | bytes 589832 | tf_op jit(solution)/shard_map/ppermute | solution.py:14
  15.8 54.9 %collective-permute-start.4 = (bf16[256,384]{1,0:T(8,128)(2,1)}, bf16[256,384]{1,0:T(8,128)(2,1)}, u32[]{:S(2)}, u32[]{:S(2)}) collective-permute-start(bf16[256,384]{1,0:T(8,128)(2,1)} %param.6), channel_id=1, source_target_pairs={{0,16},{4,20},{8,24},{12,28},{16,32},{20,36},{24,40},{28,44},{32,4... | collective-permute-start | bytes 589832 | tf_op jit(solution)/shard_map/ppermute | solution.py:14
  19.2 32.3 %collective-permute-start.1 = (bf16[256,384]{1,0:T(8,128)(2,1)}, bf16[256,384]{1,0:T(8,128)(2,1)S(1)}, u32[]{:S(2)}, u32[]{:S(2)}) collective-permute-start(bf16[256,384]{1,0:T(8,128)(2,1)} %param.7), channel_id=1, source_target_pairs={{0,12},{4,16},{8,20},{12,24},{16,28},{20,32},{24,36},{28,40},{32,4... | collective-permute-start | bytes 589832 | tf_op jit(solution)/shard_map/ppermute | solution.py:14
  22.5 26.7 %collective-permute-start = (bf16[256,384]{1,0:T(8,128)(2,1)}, bf16[256,384]{1,0:T(8,128)(2,1)}, u32[]{:S(2)}, u32[]{:S(2)}) collective-permute-start(bf16[256,384]{1,0:T(8,128)(2,1)} %param.7), channel_id=1, source_target_pairs={{0,16},{4,20},{8,24},{12,28},{16,32},{20,36},{24,40},{28,44},{32,4... | collective-permute-start | bytes 589832 | tf_op jit(solution)/shard_map/ppermute | solution.py:14
  28.3 21.0 %copy-start.23 = (bf16[256,384]{1,0:T(8,128)(2,1)S(1)}, bf16[256,384]{1,0:T(8,128)(2,1)}, u32[]{:S(2)}) copy-start(bf16[256,384]{1,0:T(8,128)(2,1)} %param.7) | copy-start | bytes 589828
  44.7 15.4 copy-start.24
  46.9 29.0 %copy-start.16 = (bf16[256,128]{0,1:T(8,128)(2,1)}, bf16[256,128]{0,1:T(8,128)(2,1)S(1)}, u32[]{:S(2)}) copy-start(bf16[256,128]{0,1:T(8,128)(2,1)S(1)} %copy.93) | copy-start | bytes 196612
  49.2 10.8 collective-permute-start.2
  51.5 17.9 %collective-permute-start.3 = (bf16[256,384]{1,0:T(8,128)(2,1)S(1)}, bf16[256,384]{1,0:T(8,128)(2,1)S(1)}, u32[]{:S(2)}, u32[]{:S(2)}) collective-permute-start(bf16[256,384]{1,0:T(8,128)(2,1)S(1)} %copy-done.23), channel_id=1, source_target_pairs={{0,4},{4,8},{8,12},{12,16},{16,20},{20,24},{24,28},{28,32},{32,36}... | collective-permute-start | bytes 589832 | tf_op jit(solution)/shard_map/ppermute | solution.py:14
  60.1 13.6 collective-permute-start.7
  80.3 1.7 copy-start.2
  82.1 1.6 copy-start.17
  83.7 4.3 copy-start.14
  91.4 2.0 copy-start.11
  93.4 1.8 copy-start.3
  95.1 1.0 copy-start.9
  95.1 2.0 copy-start.15
  97.1 5.1 copy-start.12
  105.6 2.0 copy-start.10
  107.6 1.8 copy-start.1
  109.4 1.0 copy-start.8
  109.4 1.3 copy-start.13
  115.8 2.1 copy-start.21
  115.8 2.9 copy-start.4
  116.9 2.9 copy-start.5
  116.9 4.0 copy-start.22
  117.9 3.7 copy-start.6
  119.8 3.0 copy-start.7
  127.3 63.3 %collective-permute-start.8 = (f32[256,384]{1,0:T(8,128)}, f32[256,384]{1,0:T(8,128)}, u32[]{:S(2)}, u32[]{:S(2)}) collective-permute-start(f32[256,384]{1,0:T(8,128)} %get-tuple-element.24), channel_id=1, source_target_pairs={{4,0},{8,4},{12,8},{16,12},{20,16},{24,20},{28,24},{32,28},{36,32}... | collective-permute-start | bytes 1179656 | tf_op jit(solution)/shard_map/ppermute | solution.py:14
  129.2 62.7 %collective-permute-start.11 = (f32[256,384]{1,0:T(8,128)}, f32[256,384]{1,0:T(8,128)}, u32[]{:S(2)}, u32[]{:S(2)}) collective-permute-start(f32[256,384]{1,0:T(8,128)} %get-tuple-element.25), channel_id=1, source_target_pairs={{16,0},{20,4},{24,8},{28,12},{32,16},{36,20},{40,24},{44,28},{48,3... | collective-permute-start | bytes 1179656 | tf_op jit(solution)/shard_map/ppermute | solution.py:14
  130.5 62.7 %collective-permute-start.10 = (f32[256,384]{1,0:T(8,128)}, f32[256,384]{1,0:T(8,128)}, u32[]{:S(2)}, u32[]{:S(2)}) collective-permute-start(f32[256,384]{1,0:T(8,128)} %get-tuple-element.26), channel_id=1, source_target_pairs={{12,0},{16,4},{20,8},{24,12},{28,16},{32,20},{36,24},{40,28},{44,3... | collective-permute-start | bytes 1179656 | tf_op jit(solution)/shard_map/ppermute | solution.py:14
  131.8 63.4 %collective-permute-start.9 = (f32[256,384]{1,0:T(8,128)S(1)}, f32[256,384]{1,0:T(8,128)}, u32[]{:S(2)}, u32[]{:S(2)}) collective-permute-start(f32[256,384]{1,0:T(8,128)S(1)} %get-tuple-element.27), channel_id=1, source_target_pairs={{8,0},{12,4},{16,8},{20,12},{24,16},{28,20},{32,24},{36,28},{40,32... | collective-permute-start | bytes 1179656 | tf_op jit(solution)/shard_map/ppermute | solution.py:14
  186.9 7.6 copy-start.18
  186.9 7.6 copy-start.19
  186.9 7.6 copy-start.20
  187.0 44.0 %collective-permute-start.12 = (f32[256,384]{1,0:T(8,128)S(1)}, f32[256,384]{1,0:T(8,128)S(1)}, u32[]{:S(2)}, u32[]{:S(2)}) collective-permute-start(f32[256,384]{1,0:T(8,128)S(1)} %get-tuple-element.20), channel_id=1, source_target_pairs={{4,0},{8,4},{12,8},{16,12},{20,16},{24,20},{28,24},{32,28},{36,32}... | collective-permute-start | bytes 1179656 | tf_op jit(solution)/shard_map/ppermute | solution.py:14
  190.6 52.8 %collective-permute-start.15 = (f32[256,384]{1,0:T(8,128)S(1)}, f32[256,384]{1,0:T(8,128)S(1)}, u32[]{:S(2)}, u32[]{:S(2)}) collective-permute-start(f32[256,384]{1,0:T(8,128)S(1)} %get-tuple-element.21), channel_id=1, source_target_pairs={{16,0},{20,4},{24,8},{28,12},{32,16},{36,20},{40,24},{44,28},{48,3... | collective-permute-start | bytes 1179656 | tf_op jit(solution)/shard_map/ppermute | solution.py:14
  191.9 60.6 %collective-permute-start.14 = (f32[256,384]{1,0:T(8,128)S(1)}, f32[256,384]{1,0:T(8,128)S(1)}, u32[]{:S(2)}, u32[]{:S(2)}) collective-permute-start(f32[256,384]{1,0:T(8,128)S(1)} %get-tuple-element.22), channel_id=1, source_target_pairs={{12,0},{16,4},{20,8},{24,12},{28,16},{32,20},{36,24},{40,28},{44,3... | collective-permute-start | bytes 1179656 | tf_op jit(solution)/shard_map/ppermute | solution.py:14
  193.2 65.9 %collective-permute-start.13 = (f32[256,384]{1,0:T(8,128)S(1)}, f32[256,384]{1,0:T(8,128)S(1)}, u32[]{:S(2)}, u32[]{:S(2)}) collective-permute-start(f32[256,384]{1,0:T(8,128)S(1)} %get-tuple-element.23), channel_id=1, source_target_pairs={{8,0},{12,4},{16,8},{20,12},{24,16},{28,20},{32,24},{36,28},{40,32... | collective-permute-start | bytes 1179656 | tf_op jit(solution)/shard_map/ppermute | solution.py:14
Sparse Core Ops, SparseCore 0:
  124.8 1427.4 all-reduce.3
where the time goes:
time: 1560 us
  waiting for transfers between devices  1360 us (87%)
  blocking collectives  68.6 us (4%)
  starting transfers between devices  48.1 us (3%)
  local copies, waits for them, and re-layouts  33.1 us (2%)
  matrix products  25.3 us (2%)
    unnamed x2, waiting for transfers between devices  1290 us
    ppermute x16, waiting for transfers between devices, shifted(): return lax.ppermute(block, axis, route)  65.5 us
    psum x1, blocking collectives, shards(): summed_all = lax.psum(partial_value, 'head')  52.2 us
    ppermute x16, starting transfers between devices, shifted(): return lax.ppermute(block, axis, route)  48.1 us
  transfers between devices with their start and end apart: 17, of which 7 were waited for; matrix products, arithmetic and copies ran while one was open for 1% of the time, Pallas kernels for 0%

commit v1 on v0

--- a/solution.py
+++ b/solution.py
@@ -1,8 +1,13 @@
+import functools
+
 import jax
 import jax.numpy as jnp
 from jax import lax
+from jax.experimental import pallas as pl
+from jax.experimental.pallas import tpu as pltpu
 from jax.sharding import PartitionSpec as P
 
+MESH = pl.DeviceIdType.MESH
 D = 1536
 HEADS = 24
 LOOKBACK = 4
@@ -23,6 +28,126 @@
     row_max = jnp.max(scores, axis=-1, keepdims=True)
     exp_scores = jnp.exp(scores - row_max)
     return exp_scores / jnp.sum(exp_scores, axis=-1, keepdims=True)
+
+
+X_SIZE = 4
+Y_SIZE = 4
+
+
+def weight_sum_kernel(z_size, terms_ref, out_ref, x_in, z_send, z_in, y_send, y_in, sums, x_sems, z_sems, y_sems):
+    seq = lax.axis_index("seq")
+    head = lax.axis_index("head")
+    y_at = seq % Y_SIZE
+    x_at = (seq // Y_SIZE) % X_SIZE
+    z_at = seq // (Y_SIZE * X_SIZE)
+
+    def device(z, x, y):
+        return ((z * X_SIZE + x) * Y_SIZE + y, head)
+
+    def x_peer(step):
+        return (x_at + step) % X_SIZE
+
+    def z_peer(step):
+        return (z_at + step) % z_size
+
+    def y_peer(step):
+        return (y_at + step) % Y_SIZE
+
+    barrier = pltpu.get_barrier_semaphore()
+    for step in range(1, X_SIZE):
+        pl.semaphore_signal(barrier, inc=1, device_id=device(z_at, x_peer(step), y_at), device_id_type=MESH)
+    for step in range(1, z_size):
+        pl.semaphore_signal(barrier, inc=1, device_id=device(z_peer(step), x_at, y_at), device_id_type=MESH)
+    for step in range(1, Y_SIZE):
+        pl.semaphore_signal(barrier, inc=1, device_id=device(z_at, x_at, y_peer(step)), device_id_type=MESH)
+    pl.semaphore_wait(barrier, X_SIZE + Y_SIZE + z_size - 3)
+
+    x_copies = []
+    for step in range(1, X_SIZE):
+        copy = pltpu.make_async_remote_copy(
+            src_ref=terms_ref.at[:, x_peer(step)],
+            dst_ref=x_in.at[step - 1],
+            send_sem=x_sems.at[0, step - 1],
+            recv_sem=x_sems.at[1, step - 1],
+            device_id=device(z_at, x_peer(step), y_at),
+            device_id_type=MESH,
+        )
+        copy.start()
+        x_copies.append(copy)
+    for copy in x_copies:
+        copy.wait_recv()
+    total = terms_ref[:, x_at].astype(jnp.float32)
+    for step in range(1, X_SIZE):
+        total += x_in[step - 1].astype(jnp.float32)
+    z_send[...] = total.astype(jnp.bfloat16)
+    z_copies = []
+    for step in range(1, z_size):
+        copy = pltpu.make_async_remote_copy(
+            src_ref=z_send.at[z_peer(step)],
+            dst_ref=z_in.at[step - 1],
+            send_sem=z_sems.at[0, step - 1],
+            recv_sem=z_sems.at[1, step - 1],
+            device_id=device(z_peer(step), x_at, y_at),
+            device_id_type=MESH,
+        )
+        copy.start()
+        z_copies.append(copy)
+    for copy in z_copies:
+        copy.wait_recv()
+    sums[...] = z_send[z_at].astype(jnp.float32)
+    for step in range(1, z_size):
+        sums[...] += z_in[step - 1].astype(jnp.float32)
+    rows = out_ref.shape[0]
+    for piece in range(Y_SIZE):
+        y_send[piece, 0:rows] = sums[piece * rows : (piece + 1) * rows]
+    y_copies = []
+    for step in range(1, Y_SIZE):
+        copy = pltpu.make_async_remote_copy(
+            src_ref=y_send.at[y_peer(step)],
+            dst_ref=y_in.at[step - 1],
+            send_sem=y_sems.at[0, step - 1],
+            recv_sem=y_sems.at[1, step - 1],
+            device_id=device(z_at, x_at, y_peer(step)),
+            device_id_type=MESH,
+        )
+        copy.start()
+        y_copies.append(copy)
+    result = y_send[y_at]
+    for step in range(1, Y_SIZE):
+        y_copies[step - 1].wait_recv()
+        result += y_in[step - 1]
+    out_ref[...] = result[0:rows]
+    for copy in x_copies + z_copies + y_copies:
+        copy.wait_send()
+
+
+def weight_sum(terms):
+    seq_size = lax.axis_size("seq")
+    z_size = seq_size // (X_SIZE * Y_SIZE)
+    width = terms.shape[1]
+    rows = terms.shape[0] // seq_size
+    block = rows * Y_SIZE
+    padded = (rows + 7) // 8 * 8
+    return pl.pallas_call(
+        functools.partial(weight_sum_kernel, z_size),
+        out_shape=jax.ShapeDtypeStruct((rows, width), jnp.float32),
+        in_specs=[pl.BlockSpec(memory_space=pltpu.VMEM)],
+        out_specs=pl.BlockSpec(memory_space=pltpu.VMEM),
+        scratch_shapes=[
+            pltpu.VMEM((X_SIZE - 1, z_size, block, width), jnp.bfloat16),
+            pltpu.VMEM((z_size, block, width), jnp.bfloat16),
+            pltpu.VMEM((z_size - 1, block, width), jnp.bfloat16),
+            pltpu.VMEM((Y_SIZE, padded, width), jnp.float32),
+            pltpu.VMEM((Y_SIZE - 1, padded, width), jnp.float32),
+            pltpu.VMEM((block, width), jnp.float32),
+            pltpu.SemaphoreType.DMA((2, X_SIZE - 1)),
+            pltpu.SemaphoreType.DMA((2, z_size - 1)),
+            pltpu.SemaphoreType.DMA((2, Y_SIZE - 1)),
+        ],
+        compiler_params=pltpu.CompilerParams(
+            collective_id=0, has_side_effects=True, vmem_limit_bytes=32 * 1024 * 1024
+        ),
+    )(terms.reshape(z_size, X_SIZE, block, width))
 
 
 def shards(query_rows, key_rows, value_rows, out_weight, out_grad):
@@ -139,14 +264,10 @@
         )
         key_total = key_total + arrived[0]
         value_total = value_total + arrived[1]
-    weight_grad = lax.psum_scatter(
-        lax.dot_general(
-            grad_full, attended, (((0,), (0,)), ((), ())), preferred_element_type=jnp.float32
-        ),
-        "seq",
-        scatter_dimension=0,
-        tiled=True,
-    )
+    weight_terms = lax.dot_general(
+        grad_full, attended, (((0,), (0,)), ((), ())), preferred_element_type=jnp.float32
+    )
+    weight_grad = weight_sum(weight_terms.astype(jnp.bfloat16))
     return (
         projected,
         query_grad,

time: 1560 us -> 303 us (0.19)
  the two profiles are of different devices: /device:TPU:8 before, /device:TPU:1 now
where the time goes in v1:
time: 303 us; the launch traced here: 301 us
  blocking collectives  75.8 us (25%)
  waiting for transfers between devices  69.5 us (23%)
  Pallas kernels  50.9 us (17%)
  starting transfers between devices  39.9 us (13%)
  local copies, waits for them, and re-layouts  28.8 us (10%)
  matrix products  24.9 us (8%)
  other arithmetic  9.78 us (3%)
    ppermute x16, waiting for transfers between devices, shifted(): return lax.ppermute(block, axis, route)  69.5 us
    psum x1, blocking collectives, shards(): summed_all = lax.psum(partial_value, 'head')  56.4 us
    pallas_call x1, Pallas kernels, weight_sum(): pl.pallas_call(functools.partial(weight_sum_kernel, z_size), out_shape=ja...  50.9 us
    ppermute x16, starting transfers between devices, shifted(): return lax.ppermute(block, axis, route)  39.9 us
    all_gather x1, blocking collectives, shards(): grad_full = lax.all_gather(out_grad, 'head', axis=1, tiled=True)  19.4 us
    sub x3, matrix products, window_probs(): exp_scores = jnp.exp(scores - row_max)  9.3 us
    unnamed x59, local copies, waits for them, and re-layouts  6.24 us
  transfers between devices with their start and end apart: 16, of which 7 were waited for; matrix products, arithmetic and copies ran while one was open for 3% of the time, Pallas kernels for 0%

profile of v1, /device:TPU:1, one launch (start us, length us, event | category | flops | bytes accessed | tf_op | source)
XLA Modules:
  0.0 300.7 jit_solution(8829132737376817693)
XLA Ops:
  0.6 5.9 %collective-permute-start.6 = (bf16[256,384]{1,0:T(8,128)(2,1)}, bf16[256,384]{1,0:T(8,128)(2,1)}, u32[]{:S(2)}, u32[]{:S(2)}) collective-permute-start(bf16[256,384]{1,0:T(8,128)(2,1)} %param.6), channel_id=1, source_target_pairs={{0,8},{4,12},{8,16},{12,20},{16,24},{20,28},{24,32},{28,36},{32,40... | collective-permute-start | bytes 589832 | tf_op jit(solution)/shard_map/ppermute | solution.py:19
  6.5 3.9 %collective-permute-start.5 = (bf16[256,384]{1,0:T(8,128)(2,1)}, bf16[256,384]{1,0:T(8,128)(2,1)}, u32[]{:S(2)}, u32[]{:S(2)}) collective-permute-start(bf16[256,384]{1,0:T(8,128)(2,1)} %param.6), channel_id=1, source_target_pairs={{0,12},{4,16},{8,20},{12,24},{16,28},{20,32},{24,36},{28,40},{32,4... | collective-permute-start | bytes 589832 | tf_op jit(solution)/shard_map/ppermute | solution.py:19
  10.4 3.1 %collective-permute-start.4 = (bf16[256,384]{1,0:T(8,128)(2,1)}, bf16[256,384]{1,0:T(8,128)(2,1)}, u32[]{:S(2)}, u32[]{:S(2)}) collective-permute-start(bf16[256,384]{1,0:T(8,128)(2,1)} %param.6), channel_id=1, source_target_pairs={{0,16},{4,20},{8,24},{12,28},{16,32},{20,36},{24,40},{28,44},{32,4... | collective-permute-start | bytes 589832 | tf_op jit(solution)/shard_map/ppermute | solution.py:19
  13.6 2.7 collective-permute-start.1
  16.3 3.3 %collective-permute-start = (bf16[256,384]{1,0:T(8,128)(2,1)}, bf16[256,384]{1,0:T(8,128)(2,1)S(1)}, u32[]{:S(2)}, u32[]{:S(2)}) collective-permute-start(bf16[256,384]{1,0:T(8,128)(2,1)} %param.7), channel_id=1, source_target_pairs={{0,16},{4,20},{8,24},{12,28},{16,32},{20,36},{24,40},{28,44},{32,4... | collective-permute-start | bytes 589832 | tf_op jit(solution)/shard_map/ppermute | solution.py:19
  19.5 0.9 fusion.61
  20.5 19.4 %all_gather.3 = bf16[256,1536]{1,0:T(8,128)(2,1)S(1)} all-gather(bf16[256,384]{1,0:T(8,128)(2,1)} %param.9), channel_id=1, replica_groups=mesh['seq'=128,'head'=4] {'head'}, dimensions={1}, use_global_device_ids=true | all-gather | bytes 983040 | tf_op jit(solution)/shard_map/all_gather | solution.py:207
  40.5 0.7 copy.52
  41.2 0.7 copy.60
  42.5 1.3 collective-permute-start.2
  43.8 2.2 collective-permute-start.3
  46.1 2.1 collective-permute-done.2
  48.2 7.1 %collective-permute-start.7 = (bf16[256,384]{1,0:T(8,128)(2,1)S(1)}, bf16[256,384]{1,0:T(8,128)(2,1)}, u32[]{:S(2)}, u32[]{:S(2)}) collective-permute-start(bf16[256,384]{1,0:T(8,128)(2,1)S(1)} %copy-done.24), channel_id=1, source_target_pairs={{0,4},{4,8},{8,12},{12,16},{16,20},{20,24},{24,28},{28,32},{32,36}... | collective-permute-start | bytes 589832 | tf_op jit(solution)/shard_map/ppermute | solution.py:19
  55.4 1.0 fusion.59
  56.7 0.9 constant_dynamic-update-slice_fusion.9
  57.6 1.0 constant_dynamic-update-slice_fusion.8
  58.6 1.0 constant_dynamic-update-slice_fusion.7
  59.6 1.0 constant_dynamic-update-slice_fusion.6
  60.6 1.0 fusion.58
  61.8 2.4 fusion.63
  64.3 2.0 fusion.26
  67.1 0.8 copy-done.2
  68.5 1.0 fusion.23
  70.1 1.9 copy.58
  71.9 1.9 copy.59
  73.8 3.4 %fusion.62 = (f32[2,256]{1,0:T(2,128)S(1)}, f32[2,256,1280]{1,2,0:T(8,128)}) fusion(bf16[1280,2,64]{0,2,1:T(8,128)(2,1)} %bitcast.152, bf16[256,2,64]{0,2,1:T(8,128)(2,1)S(1)} %bitcast.172, pred[1280]{0:T(1024)(128)(4,1)S(1)} %fusion.41), kind=kOutput, calls=%fused_computation.106 | convolution fusion | flops 86508800 | bytes 3017984 | tf_op jit(solution)/shard_map/sub | solution.py:29
  77.2 2.0 fusion.27
  79.6 1.4 fusion.67
  82.0 1.0 fusion.24
  82.9 1.4 convolution_multiply_fusion.3
  84.3 1.9 copy.50
  86.2 1.9 copy.51
  88.1 3.4 %fusion.64 = (f32[2,256]{1,0:T(2,128)S(1)}, f32[2,256,1280]{1,2,0:T(8,128)}) fusion(bf16[1280,2,64]{0,2,1:T(8,128)(2,1)} %bitcast.148, bf16[256,2,64]{0,2,1:T(8,128)(2,1)S(1)} %bitcast.170, pred[1280]{0:T(1024)(128)(4,1)S(1)} %fusion.41), kind=kOutput, calls=%fused_computation.108 | convolution fusion | flops 86508800 | bytes 3017984 | tf_op jit(solution)/shard_map/sub | solution.py:29
  91.5 2.0 fusion.25
  93.9 1.4 fusion.65
  96.6 1.4 convolution_multiply_fusion.5
  98.0 1.5 fusion.21
  99.5 1.8 fusion.39
  101.3 1.1 copy.84
  102.3 1.1 copy.78
  103.6 1.1 copy.85
  104.7 1.1 copy.79
  105.9 1.1 copy.83
  107.0 1.1 copy.77
  108.2 1.9 copy.86
  110.1 50.9 %shard_map.92 = f32[12,384]{1,0:T(8,128)S(1)} custom-call(bf16[8,4,48,384]{3,2,1,0:T(8,128)(2,1)S(1)} %bitcast.139), custom_call_target="tpu_custom_call" | custom-call | tf_op jit(solution)/shard_map/pallas_call | solution.py:131
  161.0 56.4 %all-reduce.1 = bf16[256,1536]{1,0:T(8,128)(2,1)S(1)} all-reduce(f32[256,1536]{1,0:T(8,128)} %fusion.39), channel_id=1, replica_groups=mesh['seq'=128,'head'=4] {'head'}, use_global_device_ids=true, to_apply=%region_6.7 | all-reduce | flops 393216 | bytes 2359296 | tf_op jit(solution)/shard_map/psum | solution.py:201
  217.4 1.4 pad_maximum_fusion
  218.9 1.4 collective-permute-start.8
  220.4 1.3 collective-permute-start.11
  221.7 1.3 collective-permute-start.10
  223.0 1.3 collective-permute-start.9
  224.6 1.3 collective-permute-start.12
  226.6 7.1 %collective-permute-done.8 = f32[256,384]{1,0:T(8,128)S(1)} collective-permute-done((f32[256,384]{1,0:T(8,128)S(1)}, f32[256,384]{1,0:T(8,128)S(1)}, u32[]{:S(2)}, u32[]{:S(2)}) %collective-permute-start.8) | collective-permute-done | bytes 393248 | tf_op jit(solution)/shard_map/ppermute | solution.py:19
  233.7 1.3 collective-permute-start.15
  235.0 9.1 %collective-permute-done.11 = f32[256,384]{1,0:T(8,128)S(1)} collective-permute-done((f32[256,384]{1,0:T(8,128)S(1)}, f32[256,384]{1,0:T(8,128)S(1)}, u32[]{:S(2)}, u32[]{:S(2)}) %collective-permute-start.11) | collective-permute-done | bytes 393248 | tf_op jit(solution)/shard_map/ppermute | solution.py:19
  244.1 1.3 collective-permute-start.14
  245.4 4.2 %collective-permute-done.10 = f32[256,384]{1,0:T(8,128)S(1)} collective-permute-done((f32[256,384]{1,0:T(8,128)S(1)}, f32[256,384]{1,0:T(8,128)S(1)}, u32[]{:S(2)}, u32[]{:S(2)}) %collective-permute-start.10) | collective-permute-done | bytes 393248 | tf_op jit(solution)/shard_map/ppermute | solution.py:19
  249.6 1.3 collective-permute-start.13
  251.6 14.1 %collective-permute-done.9 = f32[256,384]{1,0:T(8,128)S(1)} collective-permute-done((f32[256,384]{1,0:T(8,128)S(1)}, f32[256,384]{1,0:T(8,128)S(1)}, u32[]{:S(2)}, u32[]{:S(2)}) %collective-permute-start.9) | collective-permute-done | bytes 393248 | tf_op jit(solution)/shard_map/ppermute | solution.py:19
  265.6 0.8 fusion.35
  266.4 8.5 %collective-permute-done.14 = f32[256,384]{1,0:T(8,128)S(1)} collective-permute-done((f32[256,384]{1,0:T(8,128)S(1)}, f32[256,384]{1,0:T(8,128)S(1)}, u32[]{:S(2)}, u32[]{:S(2)}) %collective-permute-start.14) | collective-permute-done | bytes 393248 | tf_op jit(solution)/shard_map/ppermute | solution.py:19
  274.9 24.4 %collective-permute-done.13 = f32[256,384]{1,0:T(8,128)S(1)} collective-permute-done((f32[256,384]{1,0:T(8,128)S(1)}, f32[256,384]{1,0:T(8,128)S(1)}, u32[]{:S(2)}, u32[]{:S(2)}) %collective-permute-start.13) | collective-permute-done | bytes 393248 | tf_op jit(solution)/shard_map/ppermute | solution.py:19
  299.3 0.8 fusion.31
  (91 shorter events, 9.4 us)
Async XLA Ops:
  0.6 39.2 %copy-start = (bf16[1536,384]{1,0:T(8,128)(2,1)S(1)}, bf16[1536,384]{1,0:T(8,128)(2,1)}, u32[]{:S(2)}) copy-start(bf16[1536,384]{1,0:T(8,128)(2,1)} %param.8) | copy-start | bytes 3538948
  0.6 58.0 %collective-permute-start.6 = (bf16[256,384]{1,0:T(8,128)(2,1)}, bf16[256,384]{1,0:T(8,128)(2,1)}, u32[]{:S(2)}, u32[]{:S(2)}) collective-permute-start(bf16[256,384]{1,0:T(8,128)(2,1)} %param.6), channel_id=1, source_target_pairs={{0,8},{4,12},{8,16},{12,20},{16,24},{20,28},{24,32},{28,36},{32,40... | collective-permute-start | bytes 589832 | tf_op jit(solution)/shard_map/ppermute | solution.py:19
  6.5 51.1 %collective-permute-start.5 = (bf16[256,384]{1,0:T(8,128)(2,1)}, bf16[256,384]{1,0:T(8,128)(2,1)}, u32[]{:S(2)}, u32[]{:S(2)}) collective-permute-start(bf16[256,384]{1,0:T(8,128)(2,1)} %param.6), channel_id=1, source_target_pairs={{0,12},{4,16},{8,20},{12,24},{16,28},{20,32},{24,36},{28,40},{32,4... | collective-permute-start | bytes 589832 | tf_op jit(solution)/shard_map/ppermute | solution.py:19
  10.4 46.2 %collective-permute-start.4 = (bf16[256,384]{1,0:T(8,128)(2,1)}, bf16[256,384]{1,0:T(8,128)(2,1)}, u32[]{:S(2)}, u32[]{:S(2)}) collective-permute-start(bf16[256,384]{1,0:T(8,128)(2,1)} %param.6), channel_id=1, source_target_pairs={{0,16},{4,20},{8,24},{12,28},{16,32},{20,36},{24,40},{28,44},{32,4... | collective-permute-start | bytes 589832 | tf_op jit(solution)/shard_map/ppermute | solution.py:19
  13.6 30.3 %collective-permute-start.1 = (bf16[256,384]{1,0:T(8,128)(2,1)}, bf16[256,384]{1,0:T(8,128)(2,1)S(1)}, u32[]{:S(2)}, u32[]{:S(2)}) collective-permute-start(bf16[256,384]{1,0:T(8,128)(2,1)} %param.7), channel_id=1, source_target_pairs={{0,12},{4,16},{8,20},{12,24},{16,28},{20,32},{24,36},{28,40},{32,4... | collective-permute-start | bytes 589832 | tf_op jit(solution)/shard_map/ppermute | solution.py:19
  16.3 26.2 %collective-permute-start = (bf16[256,384]{1,0:T(8,128)(2,1)}, bf16[256,384]{1,0:T(8,128)(2,1)S(1)}, u32[]{:S(2)}, u32[]{:S(2)}) collective-permute-start(bf16[256,384]{1,0:T(8,128)(2,1)} %param.7), channel_id=1, source_target_pairs={{0,16},{4,20},{8,24},{12,28},{16,32},{20,36},{24,40},{28,44},{32,4... | collective-permute-start | bytes 589832 | tf_op jit(solution)/shard_map/ppermute | solution.py:19
  20.5 22.0 %copy-start.23 = (bf16[256,384]{1,0:T(8,128)(2,1)S(1)}, bf16[256,384]{1,0:T(8,128)(2,1)}, u32[]{:S(2)}) copy-start(bf16[256,384]{1,0:T(8,128)(2,1)} %param.7) | copy-start | bytes 589828
  39.9 8.3 %copy-start.24 = (bf16[256,384]{1,0:T(8,128)(2,1)S(1)}, bf16[256,384]{1,0:T(8,128)(2,1)}, u32[]{:S(2)}) copy-start(bf16[256,384]{1,0:T(8,128)(2,1)} %param.6) | copy-start | bytes 589828
  42.1 19.7 %copy-start.19 = (bf16[256,128]{0,1:T(8,128)(2,1)}, bf16[256,128]{0,1:T(8,128)(2,1)S(1)}, u32[]{:S(2)}) copy-start(bf16[256,128]{0,1:T(8,128)(2,1)S(1)} %copy.56) | copy-start | bytes 196612
  42.5 5.7 %collective-permute-start.2 = (bf16[256,384]{1,0:T(8,128)(2,1)S(1)}, bf16[256,384]{1,0:T(8,128)(2,1)S(1)}, u32[]{:S(2)}, u32[]{:S(2)}) collective-permute-start(bf16[256,384]{1,0:T(8,128)(2,1)S(1)} %copy-done.23), channel_id=1, source_target_pairs={{0,8},{4,12},{8,16},{12,20},{16,24},{20,28},{24,32},{28,36},{32,40... | collective-permute-start | bytes 589832 | tf_op jit(solution)/shard_map/ppermute | solution.py:19
  43.8 11.5 %collective-permute-start.3 = (bf16[256,384]{1,0:T(8,128)(2,1)S(1)}, bf16[256,384]{1,0:T(8,128)(2,1)S(1)}, u32[]{:S(2)}, u32[]{:S(2)}) collective-permute-start(bf16[256,384]{1,0:T(8,128)(2,1)S(1)} %copy-done.23), channel_id=1, source_target_pairs={{0,4},{4,8},{8,12},{12,16},{16,20},{20,24},{24,28},{28,32},{32,36}... | collective-permute-start | bytes 589832 | tf_op jit(solution)/shard_map/ppermute | solution.py:19
  48.2 11.4 %collective-permute-start.7 = (bf16[256,384]{1,0:T(8,128)(2,1)S(1)}, bf16[256,384]{1,0:T(8,128)(2,1)}, u32[]{:S(2)}, u32[]{:S(2)}) collective-permute-start(bf16[256,384]{1,0:T(8,128)(2,1)S(1)} %copy-done.24), channel_id=1, source_target_pairs={{0,4},{4,8},{8,12},{12,16},{16,20},{20,24},{24,28},{28,32},{32,36}... | collective-permute-start | bytes 589832 | tf_op jit(solution)/shard_map/ppermute | solution.py:19
  66.2 1.7 copy-start.2
  68.0 1.6 copy-start.20
  69.5 4.3 %copy-start.17 = (bf16[256,128]{0,1:T(8,128)(2,1)S(1)}, bf16[256,128]{0,1:T(8,128)(2,1)}, u32[]{:S(2)}) copy-start(bf16[256,128]{0,1:T(8,128)(2,1)} %copy.60) | copy-start | bytes 196612
  77.2 2.0 copy-start.15
  79.2 1.8 copy-start.3
  81.0 1.0 copy-start.13
  81.0 2.0 copy-start.18
  82.9 5.1 %copy-start.16 = (bf16[256,128]{0,1:T(8,128)(2,1)S(1)}, bf16[256,128]{0,1:T(8,128)(2,1)}, u32[]{:S(2)}) copy-start(bf16[256,128]{0,1:T(8,128)(2,1)} %copy.52) | copy-start | bytes 196612
  91.5 2.0 copy-start.14
  93.5 1.8 copy-start.1
  95.3 1.0 copy-start.12
  101.3 2.2 copy-start.21
  101.3 2.3 copy-start.4
  102.3 2.3 copy-start.5
  102.3 3.4 %copy-start.22 = (bf16[2,64,256]{2,1,0:T(8,128)(2,1)S(1)}, bf16[2,64,256]{2,1,0:T(8,128)(2,1)}, u32[]{:S(2)}) copy-start(bf16[2,64,256]{2,1,0:T(8,128)(2,1)} %fusion.24) | copy-start | bytes 196612
  103.4 2.5 copy-start.6
  104.7 2.3 copy-start.7
  110.1 107.3 %copy-start.11 = (f32[1280,128]{1,0:T(8,128)S(1)}, f32[1280,128]{1,0:T(8,128)}, u32[]{:S(2)}) copy-start(f32[1280,128]{1,0:T(8,128)} %copy.78) | copy-start | bytes 1966084
  218.8 5.5 %copy-start.8 = (f32[1280,128]{1,0:T(8,128)S(1)}, f32[1280,128]{1,0:T(8,128)}, u32[]{:S(2)}) copy-start(f32[1280,128]{1,0:T(8,128)} %copy.84) | copy-start | bytes 1966084
  218.8 5.5 %copy-start.9 = (f32[1280,128]{1,0:T(8,128)S(1)}, f32[1280,128]{1,0:T(8,128)}, u32[]{:S(2)}) copy-start(f32[1280,128]{1,0:T(8,128)} %copy.85) | copy-start | bytes 1966084
  218.8 5.5 %copy-start.10 = (f32[1280,128]{1,0:T(8,128)S(1)}, f32[1280,128]{1,0:T(8,128)}, u32[]{:S(2)}) copy-start(f32[1280,128]{1,0:T(8,128)} %copy.83) | copy-start | bytes 1966084
  218.9 14.7 %collective-permute-start.8 = (f32[256,384]{1,0:T(8,128)S(1)}, f32[256,384]{1,0:T(8,128)S(1)}, u32[]{:S(2)}, u32[]{:S(2)}) collective-permute-start(f32[256,384]{1,0:T(8,128)S(1)} %get-tuple-element.9), channel_id=1, source_target_pairs={{4,0},{8,4},{12,8},{16,12},{20,16},{24,20},{28,24},{32,28},{36,32}... | collective-permute-start | bytes 1179656 | tf_op jit(solution)/shard_map/ppermute | solution.py:19
  220.4 23.7 %collective-permute-start.11 = (f32[256,384]{1,0:T(8,128)S(1)}, f32[256,384]{1,0:T(8,128)S(1)}, u32[]{:S(2)}, u32[]{:S(2)}) collective-permute-start(f32[256,384]{1,0:T(8,128)S(1)} %get-tuple-element.10), channel_id=1, source_target_pairs={{16,0},{20,4},{24,8},{28,12},{32,16},{36,20},{40,24},{44,28},{48,3... | collective-permute-start | bytes 1179656 | tf_op jit(solution)/shard_map/ppermute | solution.py:19
  221.7 27.9 %collective-permute-start.10 = (f32[256,384]{1,0:T(8,128)S(1)}, f32[256,384]{1,0:T(8,128)S(1)}, u32[]{:S(2)}, u32[]{:S(2)}) collective-permute-start(f32[256,384]{1,0:T(8,128)S(1)} %get-tuple-element.11), channel_id=1, source_target_pairs={{12,0},{16,4},{20,8},{24,12},{28,16},{32,20},{36,24},{40,28},{44,3... | collective-permute-start | bytes 1179656 | tf_op jit(solution)/shard_map/ppermute | solution.py:19
  223.0 42.6 %collective-permute-start.9 = (f32[256,384]{1,0:T(8,128)S(1)}, f32[256,384]{1,0:T(8,128)S(1)}, u32[]{:S(2)}, u32[]{:S(2)}) collective-permute-start(f32[256,384]{1,0:T(8,128)S(1)} %get-tuple-element.12), channel_id=1, source_target_pairs={{8,0},{12,4},{16,8},{20,12},{24,16},{28,20},{32,24},{36,28},{40,32... | collective-permute-start | bytes 1179656 | tf_op jit(solution)/shard_map/ppermute | solution.py:19
  224.6 41.8 %collective-permute-start.12 = (f32[256,384]{1,0:T(8,128)S(1)}, f32[256,384]{1,0:T(8,128)S(1)}, u32[]{:S(2)}, u32[]{:S(2)}) collective-permute-start(f32[256,384]{1,0:T(8,128)S(1)} %get-tuple-element.5), channel_id=1, source_target_pairs={{4,0},{8,4},{12,8},{16,12},{20,16},{24,20},{28,24},{32,28},{36,32}... | collective-permute-start | bytes 1179656 | tf_op jit(solution)/shard_map/ppermute | solution.py:19
  233.7 32.7 %collective-permute-start.15 = (f32[256,384]{1,0:T(8,128)S(1)}, f32[256,384]{1,0:T(8,128)S(1)}, u32[]{:S(2)}, u32[]{:S(2)}) collective-permute-start(f32[256,384]{1,0:T(8,128)S(1)} %get-tuple-element.6), channel_id=1, source_target_pairs={{16,0},{20,4},{24,8},{28,12},{32,16},{36,20},{40,24},{44,28},{48,3... | collective-permute-start | bytes 1179656 | tf_op jit(solution)/shard_map/ppermute | solution.py:19
  244.1 30.8 %collective-permute-start.14 = (f32[256,384]{1,0:T(8,128)S(1)}, f32[256,384]{1,0:T(8,128)S(1)}, u32[]{:S(2)}, u32[]{:S(2)}) collective-permute-start(f32[256,384]{1,0:T(8,128)S(1)} %get-tuple-element.7), channel_id=1, source_target_pairs={{12,0},{16,4},{20,8},{24,12},{28,16},{32,20},{36,24},{40,28},{44,3... | collective-permute-start | bytes 1179656 | tf_op jit(solution)/shard_map/ppermute | solution.py:19
  249.6 49.8 %collective-permute-start.13 = (f32[256,384]{1,0:T(8,128)S(1)}, f32[256,384]{1,0:T(8,128)S(1)}, u32[]{:S(2)}, u32[]{:S(2)}) collective-permute-start(f32[256,384]{1,0:T(8,128)S(1)} %get-tuple-element.8), channel_id=1, source_target_pairs={{8,0},{12,4},{16,8},{20,12},{24,16},{28,20},{32,24},{36,28},{40,32... | collective-permute-start | bytes 1179656 | tf_op jit(solution)/shard_map/ppermute | solution.py:19

commit v2 on v0

v2 whole, which is shorter than its diff:
```python
import functools

import jax
import jax.numpy as jnp
from jax import lax
from jax.experimental import pallas as pl
from jax.experimental.pallas import tpu as pltpu
from jax.sharding import PartitionSpec as P

MESH = pl.DeviceIdType.MESH
BF16 = jnp.bfloat16
F32 = jnp.float32
SPAN = 256
COLS = 384
HEAD_DIM = 64
LANES = 128
HALF = 128
PIECE = SPAN + HALF
SLOTS = 6
WINDOW = 5
X_SIZE = 4
Y_SIZE = 4
HEAD_SIZE = 4
NN = (((1,), (0,)), ((), ()))
NT = (((1,), (1,)), ((), ()))
K, Q, V, DO, ATT, DQ, DK, DV = range(8)


def product(left, right, dims):
    return lax.dot_general(left, right, dims, preferred_element_type=F32)


def low_lanes(rows):
    return lax.broadcasted_iota(jnp.int32, (rows, LANES), 1) < HEAD_DIM


def swap(block):
    return pltpu.roll(block, HEAD_DIM, 1)


def fold(block):
    return jnp.where(low_lanes(HALF), block[:HALF], swap(block[HALF:]))


def to_pieces(tiles, piece_ref, scale=None):
    first, middle, last = [tile.astype(F32) for tile in tiles]
    if scale is not None:
        first, middle, last = first * scale, middle * scale, last * scale
    swapped = swap(middle)
    piece_ref[0, :SPAN] = first.astype(BF16)
    piece_ref[0, SPAN:] = jnp.where(low_lanes(HALF), middle[:HALF], swapped[HALF:]).astype(BF16)
    piece_ref[1, :SPAN] = last.astype(BF16)
    piece_ref[1, SPAN:] = jnp.where(low_lanes(HALF), swapped[:HALF], middle[HALF:]).astype(BF16)


def from_pieces(piece_ref, out_ref):
    out_ref[:, 0:LANES] = piece_ref[0, :SPAN]
    out_ref[:, 2 * LANES : 3 * LANES] = piece_ref[1, :SPAN]
    low = piece_ref[0, SPAN:].astype(F32)
    high = piece_ref[1, SPAN:].astype(F32)
    top = jnp.where(low_lanes(HALF), low, swap(high))
    bottom = jnp.where(low_lanes(HALF), swap(low), high)
    out_ref[:HALF, LANES : 2 * LANES] = top.astype(BF16)
    out_ref[HALF:, LANES : 2 * LANES] = bottom.astype(BF16)


def unfold(third):
    wide = third.astype(F32)
    return jnp.concatenate([wide, swap(wide)], axis=0)


def layer_kernel(
    z_size,
    q_ref, k_ref, v_ref, w_ref, g_ref,
    proj_ref, dq_ref, dk_ref, dv_ref, dw_ref,
    packs, q_in, do_in, k_in, v_in, att_in, dq_in, dk_in, dv_in,
    grads, grads_t, k_nat, v_nat, k_tr, v_tr, q_tr, do_tr,
    scores, weights, inverse, att_tr, dq_tr, dk_acc, dv_acc,
    back_send, back_in, attended,
    proj_send, proj_in, proj_keep, hip_send, hip_in,
    terms, x_in, z_send, z_in, y_send, y_in, sums,
    a2a_send_sems, a2a_recv_sems, flow_send_sems, flow_recv_sems, back_send_sems, back_recv_sems,
    grad_send_sems, grad_recv_sems, proj_send_sems, proj_recv_sems, x_sems, z_sems, y_sems,
):
    seq = lax.axis_index("seq")
    head = lax.axis_index("head")
    rows = z_size * X_SIZE
    y_at = seq % Y_SIZE
    row_at = seq // Y_SIZE
    x_at = row_at % X_SIZE
    z_at = row_at // X_SIZE
    core = head % 2
    high = head // 2
    y_half = y_at // 2
    y_low = y_at % 2

    def at_row(row):
        return (row % rows) * Y_SIZE + y_at

    partners = [(row_at * Y_SIZE + 2 * core + j, 2 * high + y_half) for j in range(2)]
    is_self = [(y_half == core) & (y_low == j) for j in range(2)]
    other = 2 * high + 1 - core
    after = {1: (at_row(row_at + core), other), 2: (at_row(row_at + 1), head)}
    before = {1: (at_row(row_at + rows - 1 + core), other), 2: (at_row(row_at + rows - 1), head)}
    sibling = (seq, other)
    across = (seq, 2 * (1 - high) + core)

    def x_peer(step):
        return (x_at + step) % X_SIZE

    def z_peer(step):
        return (z_at + step) % z_size

    def y_peer(step):
        return (y_at + step) % Y_SIZE

    def device(z, x, y):
        return ((z * X_SIZE + x) * Y_SIZE + y, head)

    barrier = pltpu.get_barrier_semaphore()

    def greet(target):
        pl.semaphore_signal(barrier, inc=1, device_id=target, device_id_type=MESH)

    for j in range(2):
        pl.when(jnp.logical_not(is_self[j]))(functools.partial(greet, partners[j]))
    for target in (after[1], after[2], before[1], before[2], sibling, across):
        greet(target)
    for step in range(1, X_SIZE):
        greet(device(z_at, x_peer(step), y_at))
    for step in range(1, z_size):
        greet(device(z_peer(step), x_at, y_at))
    for step in range(1, Y_SIZE):
        greet(device(z_at, x_at, y_peer(step)))

    def tiles_of(ref):
        return [ref[:, t * LANES : (t + 1) * LANES] for t in range(3)]

    to_pieces(tiles_of(k_ref), packs.at[K])
    to_pieces(tiles_of(q_ref), packs.at[Q], HEAD_DIM**-0.5)
    to_pieces(tiles_of(v_ref), packs.at[V])
    grads[head] = g_ref[...]

    greeted = X_SIZE + Y_SIZE + z_size - 3 + 8 - jnp.where(y_half == core, 1, 0)
    pl.semaphore_wait(barrier, greeted)

    started = []

    def remote(src, dst, send_sem, recv_sem, target):
        return pltpu.make_async_remote_copy(
            src_ref=src, dst_ref=dst, send_sem=send_sem, recv_sem=recv_sem, device_id=target, device_id_type=MESH
        )

    def send(*args):
        copy = remote(*args)
        copy.start()
        started.append(copy)
        return copy

    swap_waits = []

    def swap_start(kind, j, src, dst):
        copy = remote(src, dst, a2a_send_sems.at[kind, j], a2a_recv_sems.at[kind, y_low], partners[j])
        pl.when(jnp.logical_not(is_self[j]))(copy.start)
        pl.when(is_self[j])(pltpu.make_async_copy(src, dst, a2a_recv_sems.at[kind, y_low]).start)
        swap_waits.append((j, copy))

    def swap_wait(kind, j, dst):
        remote(dst, dst, a2a_send_sems.at[kind, j], a2a_recv_sems.at[kind, j], partners[j]).wait_recv()

    def grad_send(index, step, target):
        return send(grads.at[index], grads.at[index], grad_send_sems.at[step - 1], grad_recv_sems.at[step - 1], target)

    own = head
    own_across = 2 * (1 - high) + core
    from_step = {1: other, 2: own_across, 3: 2 * (1 - high) + 1 - core}

    def grad_wait(step):
        slot = grads.at[from_step[step]]
        remote(slot, slot, grad_send_sems.at[step - 1], grad_recv_sems.at[step - 1], across).wait_recv()

    grad_send(own, 2, across)
    for j in range(2):
        swap_start(K, j, packs.at[K, j], k_in.at[4 + y_low])
    grad_send(own, 1, sibling)
    for j in range(2):
        swap_start(Q, j, packs.at[Q, j], q_in.at[y_low])
    for j in range(2):
        swap_start(V, j, packs.at[V, j], v_in.at[4 + y_low])

    def flow(kind, buffer):
        for j in range(2):
            swap_wait(kind, j, buffer.at[4 + j])
            at = 0 if kind == K else 1
            for far in (2, 1):
                send(
                    buffer.at[4 + j],
                    buffer.at[4 - 2 * far + j],
                    flow_send_sems.at[at, far - 1, j],
                    flow_recv_sems.at[at, far - 1, j],
                    after[far],
                )

    def flow_wait(kind, buffer, far, j):
        at = 0 if kind == K else 1
        slot = buffer.at[4 - 2 * far + j]
        remote(
            slot, slot, flow_send_sems.at[at, far - 1, j], flow_recv_sems.at[at, far - 1, j], before[far]
        ).wait_recv()

    def spread(buffer, natural, turned, slot):
        first = buffer[slot, :SPAN]
        third = unfold(buffer[slot, SPAN:])
        natural[0, slot] = first
        natural[1, slot] = third.astype(BF16)
        turned[0, slot] = first.astype(F32).T.astype(BF16)
        turned[1, slot] = third.T.astype(BF16)

    def turn(buffer, turned, j):
        first = buffer[j, :SPAN].astype(F32).T
        third = unfold(buffer[j, SPAN:]).T
        upper = lax.broadcasted_iota(jnp.int32, (LANES, SPAN), 0) < HEAD_DIM
        turned[3 * j] = jnp.where(upper, first, 0.0).astype(BF16)
        turned[3 * j + 1] = jnp.where(upper, 0.0, first).astype(BF16)
        turned[3 * j + 2] = jnp.where(upper, third, 0.0).astype(BF16)

    flow(K, k_in)
    grad_wait(2)
    grad_send(own_across, 3, sibling)
    flow(V, v_in)
    for slot in (4, 5):
        spread(k_in, k_nat, k_tr, slot)
    for j in range(2):
        swap_wait(Q, j, q_in.at[j])
        turn(q_in, q_tr, j)
    for slot in (4, 5):
        spread(v_in, v_nat, v_tr, slot)
    grad_wait(1)
    grad_wait(3)
    acc = product(grads[0], w_ref[0:COLS], NN)
    for index in range(1, HEAD_SIZE):
        acc += product(grads[index], w_ref[index * COLS : (index + 1) * COLS], NN)
    to_pieces([acc[:, t * LANES : (t + 1) * LANES] for t in range(3)], packs.at[DO])
    for j in range(2):
        swap_start(DO, j, packs.at[DO, j], do_in.at[y_low])
    for index in range(HEAD_SIZE):
        grads_t[index] = grads[index].astype(F32).T.astype(BF16)
    for far in (1, 2):
        for j in range(2):
            flow_wait(K, k_in, far, j)
            spread(k_in, k_nat, k_tr, 4 - 2 * far + j)
    for far in (1, 2):
        for j in range(2):
            flow_wait(V, v_in, far, j)
            spread(v_in, v_nat, v_tr, 4 - 2 * far + j)

    def seen(slot):
        return (row_at > 0) | (slot >= 4 - 2 * core)

    def place(i, h):
        return h // 2, pl.multiple_of((h % 2) * HEAD_DIM, HEAD_DIM), 3 * i + h

    def forward_unit(i, h):
        tile, first, unit = place(i, h)
        query = q_tr[unit]
        top = None
        for j in range(WINDOW):
            block = product(k_nat[tile, i + j], query, NN)
            block = jnp.where(seen(i + j), block, -1e30)
            scores[j] = block
            peak = jnp.max(block, axis=0, keepdims=True)
            top = peak if top is None else jnp.maximum(top, peak)
        total = jnp.zeros((1, SPAN), F32)
        acc = jnp.zeros((HEAD_DIM, SPAN), F32)
        for j in range(WINDOW):
            part = jnp.exp(scores[j] - top)
            total += jnp.sum(part, axis=0, keepdims=True)
            part = part.astype(BF16)
            weights[unit, j] = part
            acc += product(v_tr[tile, i + j, pl.ds(first, HEAD_DIM), :], part, NN)
        share = 1.0 / total
        inverse[unit] = share
        att_tr[i, tile, pl.ds(first, HEAD_DIM), :] = acc * share

    def pack_turned(turned, kind, i):
        packs[kind, i, :SPAN] = turned[i, 0].T.astype(BF16)
        packs[kind, i, SPAN:] = fold(turned[i, 1].T).astype(BF16)

    for i in range(2):
        att_tr[i, 1] = jnp.zeros((LANES, SPAN), F32)
        dq_tr[i, 1] = jnp.zeros((LANES, SPAN), F32)
    dk_acc[...] = jnp.zeros(dk_acc.shape, F32)
    dv_acc[...] = jnp.zeros(dv_acc.shape, F32)

    for i in range(2):
        pl.loop(0, 3)(functools.partial(forward_unit, i))
        pack_turned(att_tr, ATT, i)
        swap_start(ATT, i, packs.at[ATT, i], att_in.at[y_low])

    def backward_unit(i, h):
        tile, first, unit = place(i, h)
        query = q_tr[unit]
        d_out = (do_tr[unit].astype(F32) * inverse[unit]).astype(BF16)
        do_tr[unit] = d_out
        d_half = do_tr[unit, pl.ds(first, HEAD_DIM), :].astype(F32)
        att_half = att_tr[i, tile, pl.ds(first, HEAD_DIM), :].astype(BF16).astype(F32)
        delta = jnp.sum(d_half * att_half, axis=0, keepdims=True)
        acc = jnp.zeros((HEAD_DIM, SPAN), F32)
        for j in range(WINDOW):
            part = weights[unit, j]
            d_part = product(v_nat[tile, i + j], d_out, NN)
            d_score = (part.astype(F32) * (d_part - delta)).astype(BF16)
            dk_acc[tile, i + j] += product(d_score, query, NT)
            dv_acc[tile, i + j] += product(part, d_out, NT)
            acc += product(k_tr[tile, i + j, pl.ds(first, HEAD_DIM), :], d_score, NN)
        dq_tr[i, tile, pl.ds(first, HEAD_DIM), :] = acc * (HEAD_DIM**-0.5)

    for j in range(2):
        swap_wait(DO, j, do_in.at[j])
        turn(do_in, do_tr, j)
    pl.loop(0, 3)(functools.partial(backward_unit, 0))
    pack_turned(dq_tr, DQ, 0)
    swap_start(DQ, 0, packs.at[DQ, 0], dq_in.at[y_low])

    for j in range(2):
        swap_wait(ATT, j, att_in.at[j])
    from_pieces(att_in, attended)
    att = attended[...]

    def projection(index):
        weight = w_ref[pl.ds(pl.multiple_of(index * COLS, COLS), COLS), :]
        return product(att, weight, NT)

    for at, index in enumerate((2 * (1 - high) + 1 - core, 2 * high + 1 - core)):
        proj_send[at] = projection(index).astype(BF16)
        send(proj_send.at[at], proj_in.at[at], proj_send_sems.at[at], proj_recv_sems.at[at], sibling)
    for index in range(HEAD_SIZE):
        term = product(grads_t[index], att, NN).astype(BF16)
        per_z = X_SIZE * terms.shape[2]
        for part in range(COLS // per_z):
            for x in range(X_SIZE):
                start = part * per_z + x * terms.shape[2]
                terms[index * (COLS // per_z) + part, x] = term[start : start + terms.shape[2]]
    x_copies = []
    for step in range(1, X_SIZE):
        x_copies.append(
            send(
                terms.at[:, x_peer(step)],
                x_in.at[step - 1],
                x_sems.at[0, step - 1],
                x_sems.at[1, step - 1],
                device(z_at, x_peer(step), y_at),
            )
        )
    proj_keep[0] = projection(own_across)
    proj_keep[1] = projection(own)

    pl.loop(0, 3)(functools.partial(backward_unit, 1))
    pack_turned(dq_tr, DQ, 1)
    swap_start(DQ, 1, packs.at[DQ, 1], dq_in.at[y_low])

    accs = (dk_acc, dv_acc)
    for at in range(2):
        for far in (2, 1):
            for j in range(2):
                slot = 4 - 2 * far + j
                back_send[at, slot, :SPAN] = accs[at][0, slot].astype(BF16)
                back_send[at, slot, SPAN:] = fold(accs[at][1, slot]).astype(BF16)
                send(
                    back_send.at[at, slot],
                    back_in.at[at, far - 1, j],
                    back_send_sems.at[at, far - 1, j],
                    back_recv_sems.at[at, far - 1, j],
                    before[far],
                )

    remote(proj_send.at[0], proj_in.at[0], proj_send_sems.at[0], proj_recv_sems.at[0], sibling).wait_recv()
    hip_send[...] = (proj_keep[0] + proj_in[0].astype(F32)).astype(BF16)
    hip_copy = send(hip_send, hip_in, proj_send_sems.at[2], proj_recv_sems.at[2], across)

    for copy in x_copies:
        copy.wait_recv()
    for z in range(z_size):
        total = terms[z, x_at].astype(F32)
        for step in range(1, X_SIZE):
            total += x_in[step - 1, z].astype(F32)
        z_send[z] = total.astype(BF16)
    z_copies = []
    for step in range(1, z_size):
        z_copies.append(
            send(
                z_send.at[z_peer(step)],
                z_in.at[step - 1],
                z_sems.at[0, step - 1],
                z_sems.at[1, step - 1],
                device(z_peer(step), x_at, y_at),
            )
        )

    for at in range(2):
        for j in range(2):
            tile = accs[at][0, 4 + j]
            third = fold(accs[at][1, 4 + j])
            for far in (1, 2):
                piece = back_in.at[at, far - 1, j]
                remote(
                    piece, piece, back_send_sems.at[at, far - 1, j], back_recv_sems.at[at, far - 1, j], after[far]
                ).wait_recv()
                tile += back_in[at, far - 1, j, :SPAN].astype(F32)
                third += back_in[at, far - 1, j, SPAN:].astype(F32)
            kind = (DK, DV)[at]
            packs[kind, j, :SPAN] = tile.astype(BF16)
            packs[kind, j, SPAN:] = third.astype(BF16)
            swap_start(kind, j, packs.at[kind, j], (dk_in, dv_in)[at].at[y_low])

    for copy in z_copies:
        copy.wait_recv()
    sums[...] = z_send[z_at].astype(F32)
    for step in range(1, z_size):
        sums[...] += z_in[step - 1].astype(F32)
    out_rows = dw_ref.shape[0]
    for piece in range(Y_SIZE):
        y_send[piece, 0:out_rows] = sums[piece * out_rows : (piece + 1) * out_rows]
    y_copies = []
    for step in range(1, Y_SIZE):
        y_copies.append(
            send(
                y_send.at[y_peer(step)],
                y_in.at[step - 1],
                y_sems.at[0, step - 1],
                y_sems.at[1, step - 1],
                device(z_at, x_at, y_peer(step)),
            )
        )

    for j in range(2):
        swap_wait(DQ, j, dq_in.at[j])
    from_pieces(dq_in, dq_ref)
    remote(proj_send.at[1], proj_in.at[1], proj_send_sems.at[1], proj_recv_sems.at[1], sibling).wait_recv()
    hip_copy.wait_recv()
    proj_ref[...] = (proj_keep[1] + proj_in[1].astype(F32) + hip_in[...].astype(F32)).astype(BF16)
    for j in range(2):
        swap_wait(DK, j, dk_in.at[j])
    from_pieces(dk_in, dk_ref)
    for j in range(2):
        swap_wait(DV, j, dv_in.at[j])
    from_pieces(dv_in, dv_ref)
    result = y_send[y_at]
    for step in range(1, Y_SIZE):
        y_copies[step - 1].wait_recv()
        result += y_in[step - 1]
    dw_ref[...] = result[0:out_rows]

    for copy in started:
        copy.wait_send()
    for j, copy in swap_waits:
        pl.when(jnp.logical_not(is_self[j]))(copy.wait_send)


def shards(query_rows, key_rows, value_rows, out_weight, out_grad):
    seq_size = lax.axis_size("seq")
    z_size = seq_size // (X_SIZE * Y_SIZE)
    out_rows = out_weight.shape[0] // seq_size
    block = out_rows * Y_SIZE
    padded = (out_rows + 7) // 8 * 8
    rows_out = jax.ShapeDtypeStruct((SPAN, COLS), BF16)
    vmem = pltpu.VMEM
    dma = pltpu.SemaphoreType.DMA
    piece = (PIECE, LANES)
    scratch = [
        vmem((8, 2) + piece, BF16),
        vmem((2,) + piece, BF16),
        vmem((2,) + piece, BF16),
        vmem((SLOTS,) + piece, BF16),
        vmem((SLOTS,) + piece, BF16),
        vmem((2,) + piece, BF16),
        vmem((2,) + piece, BF16),
        vmem((2,) + piece, BF16),
        vmem((2,) + piece, BF16),
        vmem((HEAD_SIZE, SPAN, COLS), BF16),
        vmem((HEAD_SIZE, COLS, SPAN), BF16),
        vmem((2, SLOTS, SPAN, LANES), BF16),
        vmem((2, SLOTS, SPAN, LANES), BF16),
        vmem((2, SLOTS, LANES, SPAN), BF16),
        vmem((2, SLOTS, LANES, SPAN), BF16),
        vmem((6, LANES, SPAN), BF16),
        vmem((6, LANES, SPAN), BF16),
        vmem((WINDOW, SPAN, SPAN), F32),
        vmem((6, WINDOW, SPAN, SPAN), BF16),
        vmem((6, 1, SPAN), F32),
        vmem((2, 2, LANES, SPAN), F32),
        vmem((2, 2, LANES, SPAN), F32),
        vmem((2, SLOTS, SPAN, LANES), F32),
        vmem((2, SLOTS, SPAN, LANES), F32),
        vmem((2, 4) + piece, BF16),
        vmem((2, 2, 2) + piece, BF16),
        vmem((SPAN, COLS), BF16),
        vmem((2, SPAN, COLS), BF16),
        vmem((2, SPAN, COLS), BF16),
        vmem((2, SPAN, COLS), F32),
        vmem((SPAN, COLS), BF16),
        vmem((SPAN, COLS), BF16),
        vmem((z_size, X_SIZE, block, COLS), BF16),
        vmem((X_SIZE - 1, z_size, block, COLS), BF16),
        vmem((z_size, block, COLS), BF16),
        vmem((z_size - 1, block, COLS), BF16),
        vmem((Y_SIZE, padded, COLS), F32),
        vmem((Y_SIZE - 1, padded, COLS), F32),
        vmem((block, COLS), F32),
        dma((8, 2)),
        dma((8, 2)),
        dma((2, 2, 2)),
        dma((2, 2, 2)),
        dma((2, 2, 2)),
        dma((2, 2, 2)),
        dma((3,)),
        dma((3,)),
        dma((3,)),
        dma((3,)),
        dma((2, X_SIZE - 1)),
        dma((2, z_size - 1)),
        dma((2, Y_SIZE - 1)),
    ]
    return pl.pallas_call(
        functools.partial(layer_kernel, z_size),
        out_shape=(rows_out,) * 4 + (jax.ShapeDtypeStruct((out_rows, COLS), F32),),
        in_specs=[pl.BlockSpec(memory_space=pltpu.VMEM)] * 5,
        out_specs=(pl.BlockSpec(memory_space=pltpu.VMEM),) * 5,
        scratch_shapes=scratch,
        compiler_params=pltpu.CompilerParams(
            collective_id=0, has_side_effects=True, vmem_limit_bytes=48 * 1024 * 1024
        ),
    )(query_rows, key_rows, value_rows, out_weight, out_grad)


def solution(mesh):
    in_specs = (
        P("seq", "head"),
        P("seq", "head"),
        P("seq", "head"),
        P(None, "head"),
        P("seq", "head"),
    )
    out_specs = (
        P("seq", "head"),
        P("seq", "head"),
        P("seq", "head"),
        P("seq", "head"),
        P("seq", "head"),
    )
    return jax.shard_map(shards, mesh=mesh, in_specs=in_specs, out_specs=out_specs, check_vma=False)
```

time: 1560 us -> 100 us (0.06)
  the two profiles are of different devices: /device:TPU:8 before, /device:TPU:31 now
where the time goes in v2:
time: 100 us
  Pallas kernels  91 us (91%)
  local copies, waits for them, and re-layouts  8.28 us (8%)
    pallas_call x1, Pallas kernels, shards(): pl.pallas_call(functools.partial(layer_kernel, z_size), out_shape=(rows_o...  91 us
    unnamed x15, local copies, waits for them, and re-layouts  8.28 us

profile of v2, /device:TPU:31, one launch (start us, length us, event | category | flops | bytes accessed | tf_op | source)
XLA Modules:
  0.0 100.0 jit_solution(17934588177006698605)
XLA Ops:
  0.6 0.0 copy-start
  0.6 1.3 %copy-done = bf16[1536,384]{1,0:T(8,128)(2,1)S(1)} copy-done((bf16[1536,384]{1,0:T(8,128)(2,1)S(1)}, bf16[1536,384]{1,0:T(8,128)(2,1)}, u32[]{:S(2)}) %copy-start) | copy-done | bytes 1179672
  1.9 0.0 copy-start.1
  1.9 0.9 copy-done.1
  2.8 0.0 copy-start.2
  2.8 0.9 copy-done.2
  3.8 0.0 copy-start.3
  3.8 0.9 copy-done.3
  4.7 0.0 copy-start.4
  4.7 0.9 copy-done.4
  5.6 91.0 %shard_map.92 = (bf16[256,384]{1,0:T(8,128)(2,1)S(1)}, bf16[256,384]{1,0:T(8,128)(2,1)S(1)}, bf16[256,384]{1,0:T(8,128)(2,1)S(1)}, bf16[256,384]{1,0:T(8,128)(2,1)S(1)}, f32[12,384]{1,0:T(8,128)S(1)}) custom-call(bf16[256,384]{1,0:T(8,128)(2,1)S(1)} %copy-done.1, bf16[256,384]{1,0:T(8,128)(2,1)S(1)} %copy-done.2, bf16[256,384]{1,0:T(8,128)(2,1)S(1)} %copy-done.3, ...), custom_call_target="tpu_custom_call" | custom-call | tf_op jit(solution)/shard_map/pallas_call | solution.py:524
  96.7 0.7 copy.15
  97.3 0.7 copy.16
  98.0 0.7 copy.17
  98.7 0.7 copy.18
  99.4 0.6 copy.19
Async XLA Ops:
  0.6 1.3 %copy-start = (bf16[1536,384]{1,0:T(8,128)(2,1)S(1)}, bf16[1536,384]{1,0:T(8,128)(2,1)}, u32[]{:S(2)}) copy-start(bf16[1536,384]{1,0:T(8,128)(2,1)} %w_ref.1) | copy-start | bytes 3538948
  1.9 0.9 copy-start.1
  2.8 0.9 copy-start.2
  3.8 0.9 copy-start.3
  4.7 0.9 copy-start.4

commit v3 on v2

--- a/solution.py
+++ b/solution.py
@@ -71,16 +71,17 @@
 
 def layer_kernel(
     z_size,
-    q_ref, k_ref, v_ref, w_ref, g_ref,
+    q_hbm, k_hbm, v_hbm, w_hbm, g_hbm,
+    proj_out, dq_out, dk_out, dv_out, dw_out,
     proj_ref, dq_ref, dk_ref, dv_ref, dw_ref,
-    packs, q_in, do_in, k_in, v_in, att_in, dq_in, dk_in, dv_in,
+    q_ref, k_ref, v_ref, w_ref, packs, q_in, do_in, k_in, v_in, att_in, dq_in, dk_in, dv_in,
     grads, grads_t, k_nat, v_nat, k_tr, v_tr, q_tr, do_tr,
     scores, weights, inverse, att_tr, dq_tr, dk_acc, dv_acc,
-    back_send, back_in, attended,
+    near_send, near_in, back_send, back_in, attended,
     proj_send, proj_in, proj_keep, hip_send, hip_in,
-    terms, x_in, z_send, z_in, y_send, y_in, sums,
-    a2a_send_sems, a2a_recv_sems, flow_send_sems, flow_recv_sems, back_send_sems, back_recv_sems,
-    grad_send_sems, grad_recv_sems, proj_send_sems, proj_recv_sems, x_sems, z_sems, y_sems,
+    x_terms, x_in, z_send, z_in, z_terms, z_first_in, x_send, x_last_in, y_send, y_in, sums,
+    load_sems, store_sems, a2a_send_sems, a2a_recv_sems, flow_sems, near_sems, back_sems, term_sems,
+    grad_send_sems, grad_recv_sems, proj_send_sems, proj_recv_sems, x_sems, z_sems, z_first_sems, x_last_sems, y_sems,
 ):
     seq = lax.axis_index("seq")
     head = lax.axis_index("head")
@@ -100,8 +101,8 @@
     partners = [(row_at * Y_SIZE + 2 * core + j, 2 * high + y_half) for j in range(2)]
     is_self = [(y_half == core) & (y_low == j) for j in range(2)]
     other = 2 * high + 1 - core
-    after = {1: (at_row(row_at + core), other), 2: (at_row(row_at + 1), head)}
-    before = {1: (at_row(row_at + rows - 1 + core), other), 2: (at_row(row_at + rows - 1), head)}
+    after = (at_row(row_at + 1), head)
+    before = (at_row(row_at + rows - 1), head)
     sibling = (seq, other)
     across = (seq, 2 * (1 - high) + core)
 
@@ -124,7 +125,7 @@
 
     for j in range(2):
         pl.when(jnp.logical_not(is_self[j]))(functools.partial(greet, partners[j]))
-    for target in (after[1], after[2], before[1], before[2], sibling, across):
+    for target in (after, before, sibling, across):
         greet(target)
     for step in range(1, X_SIZE):
         greet(device(z_at, x_peer(step), y_at))
@@ -136,15 +137,31 @@
     def tiles_of(ref):
         return [ref[:, t * LANES : (t + 1) * LANES] for t in range(3)]
 
+    loads = {}
+    for at, (name, src, dst) in enumerate(
+        (("k", k_hbm, k_ref), ("v", v_hbm, v_ref), ("q", q_hbm, q_ref), ("g", g_hbm, grads.at[head]), ("w", w_hbm, w_ref))
+    ):
+        loads[name] = pltpu.make_async_copy(src, dst, load_sems.at[at])
+        loads[name].start()
+    loads["k"].wait()
     to_pieces(tiles_of(k_ref), packs.at[K])
+    loads["v"].wait()
+    to_pieces(tiles_of(v_ref), packs.at[V])
+    loads["q"].wait()
     to_pieces(tiles_of(q_ref), packs.at[Q], HEAD_DIM**-0.5)
-    to_pieces(tiles_of(v_ref), packs.at[V])
-    grads[head] = g_ref[...]
-
-    greeted = X_SIZE + Y_SIZE + z_size - 3 + 8 - jnp.where(y_half == core, 1, 0)
+    loads["g"].wait()
+
+    greeted = X_SIZE + Y_SIZE + z_size - 3 + 6 - jnp.where(y_half == core, 1, 0)
     pl.semaphore_wait(barrier, greeted)
 
     started = []
+    stores = []
+
+    def store(src, dst):
+        copy = pltpu.make_async_copy(src, dst, store_sems.at[len(stores)])
+        copy.start()
+        stores.append(copy)
+
 
     def remote(src, dst, send_sem, recv_sem, target):
         return pltpu.make_async_remote_copy(
@@ -179,34 +196,38 @@
         slot = grads.at[from_step[step]]
         remote(slot, slot, grad_send_sems.at[step - 1], grad_recv_sems.at[step - 1], across).wait_recv()
 
-    grad_send(own, 2, across)
-    for j in range(2):
-        swap_start(K, j, packs.at[K, j], k_in.at[4 + y_low])
-    grad_send(own, 1, sibling)
+    for kind, buffer in ((K, k_in), (V, v_in)):
+        for j in range(2):
+            swap_start(kind, j, packs.at[kind, j], buffer.at[4 + y_low])
     for j in range(2):
         swap_start(Q, j, packs.at[Q, j], q_in.at[y_low])
-    for j in range(2):
-        swap_start(V, j, packs.at[V, j], v_in.at[4 + y_low])
-
-    def flow(kind, buffer):
+
+    def near_copy(at, buffer, slot, j):
+        return remote(
+            buffer.at[slot + j], buffer.at[2 + j], near_sems.at[0, at, j], near_sems.at[1, at, j], sibling
+        )
+
+    def far_copy(at, buffer, j):
+        return remote(buffer.at[4 + j], buffer.at[j], flow_sems.at[0, at, j], flow_sems.at[1, at, j], after)
+
+    def flow(at, kind, buffer):
         for j in range(2):
             swap_wait(kind, j, buffer.at[4 + j])
-            at = 0 if kind == K else 1
-            for far in (2, 1):
-                send(
-                    buffer.at[4 + j],
-                    buffer.at[4 - 2 * far + j],
-                    flow_send_sems.at[at, far - 1, j],
-                    flow_recv_sems.at[at, far - 1, j],
-                    after[far],
-                )
-
-    def flow_wait(kind, buffer, far, j):
-        at = 0 if kind == K else 1
-        slot = buffer.at[4 - 2 * far + j]
-        remote(
-            slot, slot, flow_send_sems.at[at, far - 1, j], flow_recv_sems.at[at, far - 1, j], before[far]
-        ).wait_recv()
+            copy = far_copy(at, buffer, j)
+            copy.start()
+            started.append(copy)
+            near = near_copy(at, buffer, 4, j)
+            pl.when(core == 0)(near.start)
+            started.append(near)
+
+    def flow_on(at, buffer):
+        for j in range(2):
+            remote(buffer.at[j], buffer.at[j], flow_sems.at[0, at, j], flow_sems.at[1, at, j], before).wait_recv()
+            pl.when(core == 1)(near_copy(at, buffer, 0, j).start)
+
+    def near_wait(at, buffer):
+        for j in range(2):
+            near_copy(at, buffer, 2, j).wait_recv()
 
     def spread(buffer, natural, turned, slot):
         first = buffer[slot, :SPAN]
@@ -224,35 +245,28 @@
         turned[3 * j + 1] = jnp.where(upper, 0.0, first).astype(BF16)
         turned[3 * j + 2] = jnp.where(upper, third, 0.0).astype(BF16)
 
-    flow(K, k_in)
-    grad_wait(2)
-    grad_send(own_across, 3, sibling)
-    flow(V, v_in)
+    flow(0, K, k_in)
+    flow(1, V, v_in)
+    grad_send(own, 2, across)
+    grad_send(own, 1, sibling)
     for slot in (4, 5):
         spread(k_in, k_nat, k_tr, slot)
+        spread(v_in, v_nat, v_tr, slot)
     for j in range(2):
         swap_wait(Q, j, q_in.at[j])
         turn(q_in, q_tr, j)
-    for slot in (4, 5):
+    flow_on(0, k_in)
+    for slot in (0, 1):
+        spread(k_in, k_nat, k_tr, slot)
+    flow_on(1, v_in)
+    near_wait(0, k_in)
+    for slot in (2, 3):
+        spread(k_in, k_nat, k_tr, slot)
+    for slot in (0, 1):
         spread(v_in, v_nat, v_tr, slot)
-    grad_wait(1)
-    grad_wait(3)
-    acc = product(grads[0], w_ref[0:COLS], NN)
-    for index in range(1, HEAD_SIZE):
-        acc += product(grads[index], w_ref[index * COLS : (index + 1) * COLS], NN)
-    to_pieces([acc[:, t * LANES : (t + 1) * LANES] for t in range(3)], packs.at[DO])
-    for j in range(2):
-        swap_start(DO, j, packs.at[DO, j], do_in.at[y_low])
-    for index in range(HEAD_SIZE):
-        grads_t[index] = grads[index].astype(F32).T.astype(BF16)
-    for far in (1, 2):
-        for j in range(2):
-            flow_wait(K, k_in, far, j)
-            spread(k_in, k_nat, k_tr, 4 - 2 * far + j)
-    for far in (1, 2):
-        for j in range(2):
-            flow_wait(V, v_in, far, j)
-            spread(v_in, v_nat, v_tr, 4 - 2 * far + j)
+    near_wait(1, v_in)
+    for slot in (2, 3):
+        spread(v_in, v_nat, v_tr, slot)
 
     def seen(slot):
         return (row_at > 0) | (slot >= 4 - 2 * core)
@@ -292,10 +306,26 @@
     dk_acc[...] = jnp.zeros(dk_acc.shape, F32)
     dv_acc[...] = jnp.zeros(dv_acc.shape, F32)
 
-    for i in range(2):
+    def forward(i):
         pl.loop(0, 3)(functools.partial(forward_unit, i))
         pack_turned(att_tr, ATT, i)
         swap_start(ATT, i, packs.at[ATT, i], att_in.at[y_low])
+
+    forward(0)
+    grad_wait(2)
+    grad_send(own_across, 3, sibling)
+    forward(1)
+    loads["w"].wait()
+    grad_wait(1)
+    grad_wait(3)
+    acc = product(grads[0], w_ref[0:COLS], NN)
+    for index in range(1, HEAD_SIZE):
+        acc += product(grads[index], w_ref[index * COLS : (index + 1) * COLS], NN)
+    to_pieces([acc[:, t * LANES : (t + 1) * LANES] for t in range(3)], packs.at[DO])
+    for j in range(2):
+        swap_start(DO, j, packs.at[DO, j], do_in.at[y_low])
+    for index in range(HEAD_SIZE):
+        grads_t[index] = grads[index].astype(F32).T.astype(BF16)
 
     def backward_unit(i, h):
         tile, first, unit = place(i, h)
@@ -316,13 +346,6 @@
         dq_tr[i, tile, pl.ds(first, HEAD_DIM), :] = acc * (HEAD_DIM**-0.5)
 
     for j in range(2):
-        swap_wait(DO, j, do_in.at[j])
-        turn(do_in, do_tr, j)
-    pl.loop(0, 3)(functools.partial(backward_unit, 0))
-    pack_turned(dq_tr, DQ, 0)
-    swap_start(DQ, 0, packs.at[DQ, 0], dq_in.at[y_low])
-
-    for j in range(2):
         swap_wait(ATT, j, att_in.at[j])
     from_pieces(att_in, attended)
     att = attended[...]
@@ -331,57 +354,97 @@
         weight = w_ref[pl.ds(pl.multiple_of(index * COLS, COLS), COLS), :]
         return product(att, weight, NT)
 
-    for at, index in enumerate((2 * (1 - high) + 1 - core, 2 * high + 1 - core)):
-        proj_send[at] = projection(index).astype(BF16)
-        send(proj_send.at[at], proj_in.at[at], proj_send_sems.at[at], proj_recv_sems.at[at], sibling)
+    block = x_terms.shape[2]
+    x_cols = x_terms.shape[3]
+    per_z = X_SIZE * block
     for index in range(HEAD_SIZE):
         term = product(grads_t[index], att, NN).astype(BF16)
-        per_z = X_SIZE * terms.shape[2]
         for part in range(COLS // per_z):
             for x in range(X_SIZE):
-                start = part * per_z + x * terms.shape[2]
-                terms[index * (COLS // per_z) + part, x] = term[start : start + terms.shape[2]]
+                start = part * per_z + x * block
+                z = index * (COLS // per_z) + part
+                x_terms[z, x] = term[start : start + block, :x_cols]
+                z_terms[z, x] = term[start : start + block, x_cols:]
     x_copies = []
     for step in range(1, X_SIZE):
         x_copies.append(
             send(
-                terms.at[:, x_peer(step)],
+                x_terms.at[:, x_peer(step)],
                 x_in.at[step - 1],
                 x_sems.at[0, step - 1],
                 x_sems.at[1, step - 1],
                 device(z_at, x_peer(step), y_at),
             )
         )
+    z_first_copies = []
+    for step in range(1, z_size):
+        z_first_copies.append(
+            send(
+                z_terms.at[z_peer(step)],
+                z_first_in.at[step - 1],
+                z_first_sems.at[0, step - 1],
+                z_first_sems.at[1, step - 1],
+                device(z_peer(step), x_at, y_at),
+            )
+        )
+    for at, index in enumerate((2 * (1 - high) + 1 - core, 2 * high + 1 - core)):
+        proj_send[at] = projection(index).astype(BF16)
+        send(proj_send.at[at], proj_in.at[at], proj_send_sems.at[at], proj_recv_sems.at[at], sibling)
     proj_keep[0] = projection(own_across)
     proj_keep[1] = projection(own)
 
-    pl.loop(0, 3)(functools.partial(backward_unit, 1))
-    pack_turned(dq_tr, DQ, 1)
-    swap_start(DQ, 1, packs.at[DQ, 1], dq_in.at[y_low])
+    for j in range(2):
+        swap_wait(DO, j, do_in.at[j])
+        turn(do_in, do_tr, j)
+    for i in range(2):
+        pl.loop(0, 3)(functools.partial(backward_unit, i))
+        pack_turned(dq_tr, DQ, i)
+        swap_start(DQ, i, packs.at[DQ, i], dq_in.at[y_low])
+        if i == 0:
+            remote(proj_send.at[0], proj_in.at[0], proj_send_sems.at[0], proj_recv_sems.at[0], sibling).wait_recv()
+            hip_send[...] = (proj_keep[0] + proj_in[0].astype(F32)).astype(BF16)
+            hip_copy = send(hip_send, hip_in, proj_send_sems.at[2], proj_recv_sems.at[2], across)
 
     accs = (dk_acc, dv_acc)
+
+    def term_copy(at, j):
+        return remote(
+            near_send.at[at, j], near_in.at[at, j], term_sems.at[0, at, j], term_sems.at[1, at, j], sibling
+        )
+
+    def back_copy(at, j, target):
+        return remote(
+            back_send.at[at, j], back_in.at[at, j], back_sems.at[0, at, j], back_sems.at[1, at, j], target
+        )
+
+    def send_back(summed):
+        for at in range(2):
+            for j in range(2):
+                tile = accs[at][0, j]
+                third = fold(accs[at][1, j])
+                if summed:
+                    term_copy(at, j).wait_recv()
+                    tile += near_in[at, j, :SPAN].astype(F32)
+                    third += near_in[at, j, SPAN:].astype(F32)
+                back_send[at, j, :SPAN] = tile.astype(BF16)
+                back_send[at, j, SPAN:] = third.astype(BF16)
+                back_copy(at, j, before).start()
+
     for at in range(2):
-        for far in (2, 1):
-            for j in range(2):
-                slot = 4 - 2 * far + j
-                back_send[at, slot, :SPAN] = accs[at][0, slot].astype(BF16)
-                back_send[at, slot, SPAN:] = fold(accs[at][1, slot]).astype(BF16)
-                send(
-                    back_send.at[at, slot],
-                    back_in.at[at, far - 1, j],
-                    back_send_sems.at[at, far - 1, j],
-                    back_recv_sems.at[at, far - 1, j],
-                    before[far],
-                )
-
-    remote(proj_send.at[0], proj_in.at[0], proj_send_sems.at[0], proj_recv_sems.at[0], sibling).wait_recv()
-    hip_send[...] = (proj_keep[0] + proj_in[0].astype(F32)).astype(BF16)
-    hip_copy = send(hip_send, hip_in, proj_send_sems.at[2], proj_recv_sems.at[2], across)
+        for j in range(2):
+            near_send[at, j, :SPAN] = accs[at][0, 2 + j].astype(BF16)
+            near_send[at, j, SPAN:] = fold(accs[at][1, 2 + j]).astype(BF16)
+            copy = term_copy(at, j)
+            copy.start()
+            started.append(copy)
+            started.append(back_copy(at, j, before))
+    pl.when(core == 0)(functools.partial(send_back, False))
+    pl.when(core == 1)(functools.partial(send_back, True))
 
     for copy in x_copies:
         copy.wait_recv()
     for z in range(z_size):
-        total = terms[z, x_at].astype(F32)
+        total = x_terms[z, x_at].astype(F32)
         for step in range(1, X_SIZE):
             total += x_in[step - 1, z].astype(F32)
         z_send[z] = total.astype(BF16)
@@ -396,28 +459,64 @@
                 device(z_peer(step), x_at, y_at),
             )
         )
-
-    for at in range(2):
+    for copy in z_first_copies:
+        copy.wait_recv()
+    for x in range(X_SIZE):
+        total = z_terms[z_at, x].astype(F32)
+        for step in range(1, z_size):
+            total += z_first_in[step - 1, x].astype(F32)
+        x_send[x] = total.astype(BF16)
+    x_last_copies = []
+    for step in range(1, X_SIZE):
+        x_last_copies.append(
+            send(
+                x_send.at[x_peer(step)],
+                x_last_in.at[step - 1],
+                x_last_sems.at[0, step - 1],
+                x_last_sems.at[1, step - 1],
+                device(z_at, x_peer(step), y_at),
+            )
+        )
+
+    def finish(near):
+        for at in range(2):
+            for j in range(2):
+                tile = accs[at][0, 4 + j]
+                third = fold(accs[at][1, 4 + j])
+                if near:
+                    term_copy(at, j).wait_recv()
+                    tile += near_in[at, j, :SPAN].astype(F32)
+                    third += near_in[at, j, SPAN:].astype(F32)
+                back_copy(at, j, after).wait_recv()
+                tile += back_in[at, j, :SPAN].astype(F32)
+                third += back_in[at, j, SPAN:].astype(F32)
+                kind = (DK, DV)[at]
+                packs[kind, j, :SPAN] = tile.astype(BF16)
+                packs[kind, j, SPAN:] = third.astype(BF16)
+                swap_start(kind, j, packs.at[kind, j], (dk_in, dv_in)[at].at[y_low])
+
+    finish_waits = len(swap_waits)
+    pl.when(core == 0)(functools.partial(finish, True))
+    del swap_waits[finish_waits:]
+    pl.when(core == 1)(functools.partial(finish, False))
+    del swap_waits[finish_waits:]
+    for kind, buffer in ((DK, dk_in), (DV, dv_in)):
         for j in range(2):
-            tile = accs[at][0, 4 + j]
-            third = fold(accs[at][1, 4 + j])
-            for far in (1, 2):
-                piece = back_in.at[at, far - 1, j]
-                remote(
-                    piece, piece, back_send_sems.at[at, far - 1, j], back_recv_sems.at[at, far - 1, j], after[far]
-                ).wait_recv()
-                tile += back_in[at, far - 1, j, :SPAN].astype(F32)
-                third += back_in[at, far - 1, j, SPAN:].astype(F32)
-            kind = (DK, DV)[at]
-            packs[kind, j, :SPAN] = tile.astype(BF16)
-            packs[kind, j, SPAN:] = third.astype(BF16)
-            swap_start(kind, j, packs.at[kind, j], (dk_in, dv_in)[at].at[y_low])
+            src = packs.at[kind, j]
+            swap_waits.append(
+                (j, remote(src, src, a2a_send_sems.at[kind, j], a2a_recv_sems.at[kind, y_low], partners[j]))
+            )
 
     for copy in z_copies:
         copy.wait_recv()
-    sums[...] = z_send[z_at].astype(F32)
+    sums[:, :x_cols] = z_send[z_at].astype(F32)
     for step in range(1, z_size):
-        sums[...] += z_in[step - 1].astype(F32)
+        sums[:, :x_cols] += z_in[step - 1].astype(F32)
+    for copy in x_last_copies:
+        copy.wait_recv()
+    sums[:, x_cols:] = x_send[x_at].astype(F32)
+    for step in range(1, X_SIZE):
+        sums[:, x_cols:] += x_last_in[step - 1].astype(F32)
     out_rows = dw_ref.shape[0]
     for piece in range(Y_SIZE):
         y_send[piece, 0:out_rows] = sums[piece * out_rows : (piece + 1) * out_rows]
@@ -436,25 +535,47 @@
     for j in range(2):
         swap_wait(DQ, j, dq_in.at[j])
     from_pieces(dq_in, dq_ref)
+    store(dq_ref, dq_out)
     remote(proj_send.at[1], proj_in.at[1], proj_send_sems.at[1], proj_recv_sems.at[1], sibling).wait_recv()
     hip_copy.wait_recv()
     proj_ref[...] = (proj_keep[1] + proj_in[1].astype(F32) + hip_in[...].astype(F32)).astype(BF16)
+    store(proj_ref, proj_out)
     for j in range(2):
         swap_wait(DK, j, dk_in.at[j])
     from_pieces(dk_in, dk_ref)
+    store(dk_ref, dk_out)
     for j in range(2):
         swap_wait(DV, j, dv_in.at[j])
     from_pieces(dv_in, dv_ref)
+    store(dv_ref, dv_out)
     result = y_send[y_at]
     for step in range(1, Y_SIZE):
         y_copies[step - 1].wait_recv()
         result += y_in[step - 1]
     dw_ref[...] = result[0:out_rows]
+    store(dw_ref, dw_out)
 
     for copy in started:
         copy.wait_send()
     for j, copy in swap_waits:
         pl.when(jnp.logical_not(is_self[j]))(copy.wait_send)
+    for copy in stores:
+        copy.wait()
+
+
+def results_kernel(*refs):
+    sems = refs[-1]
+    count = (len(refs) - 1) // 3
+    sources, targets, held = refs[:count], refs[count : 2 * count], refs[2 * count : 3 * count]
+    loads = [pltpu.make_async_copy(sources[at], held[at], sems.at[0, at]) for at in range(count)]
+    stores = [pltpu.make_async_copy(held[at], targets[at], sems.at[1, at]) for at in range(count)]
+    for copy in loads:
+        copy.start()
+    for load, copy in zip(loads, stores):
+        load.wait()
+        copy.start()
+    for copy in stores:
+        copy.wait()
 
 
 def shards(query_rows, key_rows, value_rows, out_weight, out_grad):
@@ -463,11 +584,21 @@
     out_rows = out_weight.shape[0] // seq_size
     block = out_rows * Y_SIZE
     padded = (out_rows + 7) // 8 * 8
+    x_cols = 2 * LANES
     rows_out = jax.ShapeDtypeStruct((SPAN, COLS), BF16)
     vmem = pltpu.VMEM
     dma = pltpu.SemaphoreType.DMA
     piece = (PIECE, LANES)
     scratch = [
+        vmem((SPAN, COLS), BF16),
+        vmem((SPAN, COLS), BF16),
+        vmem((SPAN, COLS), BF16),
+        vmem((SPAN, COLS), BF16),
+        vmem((out_rows, COLS), F32),
+        vmem((SPAN, COLS), BF16),
+        vmem((SPAN, COLS), BF16),
+        vmem((SPAN, COLS), BF16),
+        vmem(out_weight.shape, BF16),
         vmem((8, 2) + piece, BF16),
         vmem((2,) + piece, BF16),
         vmem((2,) + piece, BF16),
@@ -492,21 +623,29 @@
         vmem((2, 2, LANES, SPAN), F32),
         vmem((2, SLOTS, SPAN, LANES), F32),
         vmem((2, SLOTS, SPAN, LANES), F32),
-        vmem((2, 4) + piece, BF16),
-        vmem((2, 2, 2) + piece, BF16),
+        vmem((2, 2) + piece, BF16),
+        vmem((2, 2) + piece, BF16),
+        vmem((2, 2) + piece, BF16),
+        vmem((2, 2) + piece, BF16),
         vmem((SPAN, COLS), BF16),
         vmem((2, SPAN, COLS), BF16),
         vmem((2, SPAN, COLS), BF16),
         vmem((2, SPAN, COLS), F32),
         vmem((SPAN, COLS), BF16),
         vmem((SPAN, COLS), BF16),
-        vmem((z_size, X_SIZE, block, COLS), BF16),
-        vmem((X_SIZE - 1, z_size, block, COLS), BF16),
-        vmem((z_size, block, COLS), BF16),
-        vmem((z_size - 1, block, COLS), BF16),
+        vmem((z_size, X_SIZE, block, x_cols), BF16),
+        vmem((X_SIZE - 1, z_size, block, x_cols), BF16),
+        vmem((z_size, block, x_cols), BF16),
+        vmem((z_size - 1, block, x_cols), BF16),
+        vmem((z_size, X_SIZE, block, COLS - x_cols), BF16),
+        vmem((z_size - 1, X_SIZE, block, COLS - x_cols), BF16),
+        vmem((X_SIZE, block, COLS - x_cols), BF16),
+        vmem((X_SIZE - 1, block, COLS - x_cols), BF16),
         vmem((Y_SIZE, padded, COLS), F32),
         vmem((Y_SIZE - 1, padded, COLS), F32),
         vmem((block, COLS), F32),
+        dma((5,)),
+        dma((5,)),
         dma((8, 2)),
         dma((8, 2)),
         dma((2, 2, 2)),
@@ -519,18 +658,30 @@
         dma((3,)),
         dma((2, X_SIZE - 1)),
         dma((2, z_size - 1)),
+        dma((2, z_size - 1)),
+        dma((2, X_SIZE - 1)),
         dma((2, Y_SIZE - 1)),
     ]
-    return pl.pallas_call(
+    outputs = (rows_out,) * 4 + (jax.ShapeDtypeStruct((out_rows, COLS), F32),)
+    anywhere = pl.BlockSpec(memory_space=pl.ANY)
+    results = pl.pallas_call(
         functools.partial(layer_kernel, z_size),
-        out_shape=(rows_out,) * 4 + (jax.ShapeDtypeStruct((out_rows, COLS), F32),),
-        in_specs=[pl.BlockSpec(memory_space=pltpu.VMEM)] * 5,
-        out_specs=(pl.BlockSpec(memory_space=pltpu.VMEM),) * 5,
+        out_shape=outputs,
+        in_specs=[anywhere] * 5,
+        out_specs=(anywhere,) * 5,
         scratch_shapes=scratch,
         compiler_params=pltpu.CompilerParams(
-            collective_id=0, has_side_effects=True, vmem_limit_bytes=48 * 1024 * 1024
+            collective_id=0, has_side_effects=True, vmem_limit_bytes=60 * 1024 * 1024
         ),
     )(query_rows, key_rows, value_rows, out_weight, out_grad)
+    return pl.pallas_call(
+        results_kernel,
+        out_shape=outputs,
+        in_specs=[anywhere] * 5,
+        out_specs=(anywhere,) * 5,
+        scratch_shapes=[vmem(kept.shape, kept.dtype) for kept in outputs] + [dma((2, 5))],
+        compiler_params=pltpu.CompilerParams(vmem_limit_bytes=60 * 1024 * 1024),
+    )(*results)
 
 
 def solution(mesh):

time: 100 us -> 82.5 us (0.82)
  the two profiles are of different devices: /device:TPU:31 before, /device:TPU:1 now
where the time goes in v3:
time: 82.5 us; the launch traced here: 82.4 us
  Pallas kernels  81.7 us (99%)
    pallas_call x1, Pallas kernels, shards(): pl.pallas_call(functools.partial(layer_kernel, z_size), out_shape=outputs...  79.7 us
    pallas_call x1, Pallas kernels, shards(): pl.pallas_call(results_kernel, out_shape=outputs, in_specs=[anywhere] * 5...  1.99 us

profile of v3, /device:TPU:1, one launch (start us, length us, event | category | flops | bytes accessed | tf_op | source)
XLA Modules:
  0.0 82.4 jit_solution(9113618527685038480)
XLA Ops:
  0.6 79.7 %shard_map.92 = (bf16[256,384]{1,0:T(8,128)(2,1)}, bf16[256,384]{1,0:T(8,128)(2,1)}, bf16[256,384]{1,0:T(8,128)(2,1)}, bf16[256,384]{1,0:T(8,128)(2,1)}, f32[12,384]{1,0:T(8,128)}) custom-call(bf16[256,384]{1,0:T(8,128)(2,1)} %q_hbm.1, bf16[256,384]{1,0:T(8,128)(2,1)} %k_hbm.1, bf16[256,384]{1,0:T(8,128)(2,1)} %v_hbm.1, bf16[1536,384]{1,0:T(8,128)(2,1)} %w_hbm.1, ...), custom_call_target="tpu_custom_call" | custom-call | tf_op jit(solution)/shard_map/pallas_call | solution.py:667
  80.4 2.0 %shard_map.93 = (bf16[256,384]{1,0:T(8,128)(2,1)}, bf16[256,384]{1,0:T(8,128)(2,1)}, bf16[256,384]{1,0:T(8,128)(2,1)}, bf16[256,384]{1,0:T(8,128)(2,1)}, f32[12,384]{1,0:T(8,128)}) custom-call(bf16[256,384]{1,0:T(8,128)(2,1)} %get-tuple-element.10.refs_0_, bf16[256,384]{1,0:T(8,128)(2,1)} %get-tuple-element.11.refs_1_, ...), custom_call_target="tpu_custom_call" | custom-call | tf_op jit(solution)/shard_map/pallas_call | solution.py:677

commit v4 on v3

--- a/solution.py
+++ b/solution.py
@@ -106,6 +106,9 @@
     sibling = (seq, other)
     across = (seq, 2 * (1 - high) + core)
 
+    has_after = row_at < rows - 1
+    has_before = row_at > 0
+
     def x_peer(step):
         return (x_at + step) % X_SIZE
 
@@ -125,8 +128,10 @@
 
     for j in range(2):
         pl.when(jnp.logical_not(is_self[j]))(functools.partial(greet, partners[j]))
-    for target in (after, before, sibling, across):
-        greet(target)
+    pl.when(has_after)(functools.partial(greet, after))
+    pl.when(has_before)(functools.partial(greet, before))
+    greet(sibling)
+    greet(across)
     for step in range(1, X_SIZE):
         greet(device(z_at, x_peer(step), y_at))
     for step in range(1, z_size):
@@ -151,7 +156,22 @@
     to_pieces(tiles_of(q_ref), packs.at[Q], HEAD_DIM**-0.5)
     loads["g"].wait()
 
+    @pl.when(jnp.logical_not(has_before))
+    def _():
+        k_in[0:2] = jnp.zeros((2, PIECE, LANES), BF16)
+        v_in[0:2] = jnp.zeros((2, PIECE, LANES), BF16)
+
+    @pl.when(jnp.logical_not(has_before) & (core == 0))
+    def _():
+        k_in[2:4] = jnp.zeros((2, PIECE, LANES), BF16)
+        v_in[2:4] = jnp.zeros((2, PIECE, LANES), BF16)
+
+    @pl.when(jnp.logical_not(has_after))
+    def _():
+        back_in[...] = jnp.zeros(back_in.shape, BF16)
+
     greeted = X_SIZE + Y_SIZE + z_size - 3 + 6 - jnp.where(y_half == core, 1, 0)
+    greeted -= jnp.where(has_after, 0, 1) + jnp.where(has_before, 0, 1)
     pl.semaphore_wait(barrier, greeted)
 
     started = []
@@ -174,13 +194,13 @@
         started.append(copy)
         return copy
 
-    swap_waits = []
+    waits = []
 
     def swap_start(kind, j, src, dst):
         copy = remote(src, dst, a2a_send_sems.at[kind, j], a2a_recv_sems.at[kind, y_low], partners[j])
         pl.when(jnp.logical_not(is_self[j]))(copy.start)
         pl.when(is_self[j])(pltpu.make_async_copy(src, dst, a2a_recv_sems.at[kind, y_low]).start)
-        swap_waits.append((j, copy))
+        waits.append((jnp.logical_not(is_self[j]), copy.wait_send))
 
     def swap_wait(kind, j, dst):
         remote(dst, dst, a2a_send_sems.at[kind, j], a2a_recv_sems.at[kind, j], partners[j]).wait_recv()
@@ -213,21 +233,23 @@
     def flow(at, kind, buffer):
         for j in range(2):
             swap_wait(kind, j, buffer.at[4 + j])
-            copy = far_copy(at, buffer, j)
-            copy.start()
-            started.append(copy)
+            far = far_copy(at, buffer, j)
+            pl.when(has_after)(far.start)
+            waits.append((has_after, far.wait_send))
             near = near_copy(at, buffer, 4, j)
             pl.when(core == 0)(near.start)
-            started.append(near)
+            waits.append(((core == 0) | has_before, near.wait_send))
 
     def flow_on(at, buffer):
         for j in range(2):
-            remote(buffer.at[j], buffer.at[j], flow_sems.at[0, at, j], flow_sems.at[1, at, j], before).wait_recv()
-            pl.when(core == 1)(near_copy(at, buffer, 0, j).start)
+            pl.when(has_before)(
+                remote(buffer.at[j], buffer.at[j], flow_sems.at[0, at, j], flow_sems.at[1, at, j], before).wait_recv
+            )
+            pl.when((core == 1) & has_before)(near_copy(at, buffer, 0, j).start)
 
     def near_wait(at, buffer):
         for j in range(2):
-            near_copy(at, buffer, 2, j).wait_recv()
+            pl.when((core == 1) | has_before)(near_copy(at, buffer, 2, j).wait_recv)
 
     def spread(buffer, natural, turned, slot):
         first = buffer[slot, :SPAN]
@@ -428,7 +450,7 @@
                     third += near_in[at, j, SPAN:].astype(F32)
                 back_send[at, j, :SPAN] = tile.astype(BF16)
                 back_send[at, j, SPAN:] = third.astype(BF16)
-                back_copy(at, j, before).start()
+                pl.when(has_before)(back_copy(at, j, before).start)
 
     for at in range(2):
         for j in range(2):
@@ -437,7 +459,7 @@
             copy = term_copy(at, j)
             copy.start()
             started.append(copy)
-            started.append(back_copy(at, j, before))
+            waits.append((has_before, back_copy(at, j, before).wait_send))
     pl.when(core == 0)(functools.partial(send_back, False))
     pl.when(core == 1)(functools.partial(send_back, True))
 
@@ -487,7 +509,7 @@
                     term_copy(at, j).wait_recv()
                     tile += near_in[at, j, :SPAN].astype(F32)
                     third += near_in[at, j, SPAN:].astype(F32)
-                back_copy(at, j, after).wait_recv()
+                pl.when(has_after)(back_copy(at, j, after).wait_recv)
                 tile += back_in[at, j, :SPAN].astype(F32)
                 third += back_in[at, j, SPAN:].astype(F32)
                 kind = (DK, DV)[at]
@@ -495,17 +517,16 @@
                 packs[kind, j, SPAN:] = third.astype(BF16)
                 swap_start(kind, j, packs.at[kind, j], (dk_in, dv_in)[at].at[y_low])
 
-    finish_waits = len(swap_waits)
+    finish_waits = len(waits)
     pl.when(core == 0)(functools.partial(finish, True))
-    del swap_waits[finish_waits:]
+    del waits[finish_waits:]
     pl.when(core == 1)(functools.partial(finish, False))
-    del swap_waits[finish_waits:]
+    del waits[finish_waits:]
     for kind, buffer in ((DK, dk_in), (DV, dv_in)):
         for j in range(2):
             src = packs.at[kind, j]
-            swap_waits.append(
-                (j, remote(src, src, a2a_send_sems.at[kind, j], a2a_recv_sems.at[kind, y_low], partners[j]))
-            )
+            copy = remote(src, src, a2a_send_sems.at[kind, j], a2a_recv_sems.at[kind, y_low], partners[j])
+            waits.append((jnp.logical_not(is_self[j]), copy.wait_send))
 
     for copy in z_copies:
         copy.wait_recv()
@@ -557,8 +578,8 @@
 
     for copy in started:
         copy.wait_send()
-    for j, copy in swap_waits:
-        pl.when(jnp.logical_not(is_self[j]))(copy.wait_send)
+    for sent, wait in waits:
+        pl.when(sent)(wait)
     for copy in stores:
         copy.wait()
 

time: 82.5 us -> 79.3 us (0.961)
  Pallas kernels: 81.7 us -> 78 us
    pallas_call x1, Pallas kernels: 79.7 us -> 76 us  [shards(): pl.pallas_call(functools.partial(layer_kernel, z_size), out_shape=outputs...]
where the time goes in v4:
time: 79.3 us; the launch traced here: 78.6 us
  Pallas kernels  78 us (98%)
    pallas_call x1, Pallas kernels, shards(): pl.pallas_call(functools.partial(layer_kernel, z_size), out_shape=outputs...  76 us
    pallas_call x1, Pallas kernels, shards(): pl.pallas_call(results_kernel, out_shape=outputs, in_specs=[anywhere] * 5...  1.99 us

profile of v4, /device:TPU:1, one launch (start us, length us, event | category | flops | bytes accessed | tf_op | source)
XLA Modules:
  0.0 78.6 jit_solution(2028613930054903281)
XLA Ops:
  0.6 76.0 %shard_map.92 = (bf16[256,384]{1,0:T(8,128)(2,1)}, bf16[256,384]{1,0:T(8,128)(2,1)}, bf16[256,384]{1,0:T(8,128)(2,1)}, bf16[256,384]{1,0:T(8,128)(2,1)}, f32[12,384]{1,0:T(8,128)}) custom-call(bf16[256,384]{1,0:T(8,128)(2,1)} %q_hbm.1, bf16[256,384]{1,0:T(8,128)(2,1)} %k_hbm.1, bf16[256,384]{1,0:T(8,128)(2,1)} %v_hbm.1, bf16[1536,384]{1,0:T(8,128)(2,1)} %w_hbm.1, ...), custom_call_target="tpu_custom_call" | custom-call | tf_op jit(solution)/shard_map/pallas_call | solution.py:688
  76.6 2.0 %shard_map.93 = (bf16[256,384]{1,0:T(8,128)(2,1)}, bf16[256,384]{1,0:T(8,128)(2,1)}, bf16[256,384]{1,0:T(8,128)(2,1)}, bf16[256,384]{1,0:T(8,128)(2,1)}, f32[12,384]{1,0:T(8,128)}) custom-call(bf16[256,384]{1,0:T(8,128)(2,1)} %get-tuple-element.10.refs_0_, bf16[256,384]{1,0:T(8,128)(2,1)} %get-tuple-element.11.refs_1_, ...), custom_call_target="tpu_custom_call" | custom-call | tf_op jit(solution)/shard_map/pallas_call | solution.py:698

commit v5 on v4

--- a/solution.py
+++ b/solution.py
@@ -586,16 +586,11 @@
 
 def results_kernel(*refs):
     sems = refs[-1]
-    count = (len(refs) - 1) // 3
-    sources, targets, held = refs[:count], refs[count : 2 * count], refs[2 * count : 3 * count]
-    loads = [pltpu.make_async_copy(sources[at], held[at], sems.at[0, at]) for at in range(count)]
-    stores = [pltpu.make_async_copy(held[at], targets[at], sems.at[1, at]) for at in range(count)]
-    for copy in loads:
+    count = (len(refs) - 1) // 2
+    copies = [pltpu.make_async_copy(refs[at], refs[count + at], sems.at[at]) for at in range(count)]
+    for copy in copies:
         copy.start()
-    for load, copy in zip(loads, stores):
-        load.wait()
-        copy.start()
-    for copy in stores:
+    for copy in copies:
         copy.wait()
 
 
@@ -692,16 +687,16 @@
         out_specs=(anywhere,) * 5,
         scratch_shapes=scratch,
         compiler_params=pltpu.CompilerParams(
-            collective_id=0, has_side_effects=True, vmem_limit_bytes=60 * 1024 * 1024
+            collective_id=0, has_side_effects=True, vmem_limit_bytes=53 * 1024 * 1024
         ),
     )(query_rows, key_rows, value_rows, out_weight, out_grad)
     return pl.pallas_call(
         results_kernel,
         out_shape=outputs,
-        in_specs=[anywhere] * 5,
+        in_specs=[pl.BlockSpec(memory_space=pltpu.VMEM)] * 5,
         out_specs=(anywhere,) * 5,
-        scratch_shapes=[vmem(kept.shape, kept.dtype) for kept in outputs] + [dma((2, 5))],
-        compiler_params=pltpu.CompilerParams(vmem_limit_bytes=60 * 1024 * 1024),
+        scratch_shapes=[dma((5,))],
+        compiler_params=pltpu.CompilerParams(vmem_limit_bytes=4 * 1024 * 1024),
     )(*results)
 
 

time: 79.3 us -> 77.7 us (0.980)
  Pallas kernels: 78 us -> 76.4 us
    pallas_call x1, Pallas kernels: 1.99 us -> 0.92 us  [shards(): pl.pallas_call(results_kernel, out_shape=outputs, in_specs=[pl.BlockSpec(...]
where the time goes in v5:
time: 77.7 us; the launch traced here: 77 us
  Pallas kernels  76.4 us (98%)
    pallas_call x1, Pallas kernels, shards(): pl.pallas_call(functools.partial(layer_kernel, z_size), out_shape=outputs...  75.5 us

profile of v5, /device:TPU:1, one launch (start us, length us, event | category | flops | bytes accessed | tf_op | source)
XLA Modules:
  0.0 77.0 jit_solution(6334589901067989529)
XLA Ops:
  0.6 75.5 %shard_map.92 = (bf16[256,384]{1,0:T(8,128)(2,1)S(1)}, bf16[256,384]{1,0:T(8,128)(2,1)S(1)}, bf16[256,384]{1,0:T(8,128)(2,1)S(1)}, bf16[256,384]{1,0:T(8,128)(2,1)S(1)}, f32[12,384]{1,0:T(8,128)S(1)}) custom-call(bf16[256,384]{1,0:T(8,128)(2,1)} %q_hbm.1, bf16[256,384]{1,0:T(8,128)(2,1)} %k_hbm.1, bf16[256,384]{1,0:T(8,128)(2,1)} %v_hbm.1, ...), custom_call_target="tpu_custom_call" | custom-call | tf_op jit(solution)/shard_map/pallas_call | solution.py:683
  76.1 0.9 %shard_map.93 = (bf16[256,384]{1,0:T(8,128)(2,1)}, bf16[256,384]{1,0:T(8,128)(2,1)}, bf16[256,384]{1,0:T(8,128)(2,1)}, bf16[256,384]{1,0:T(8,128)(2,1)}, f32[12,384]{1,0:T(8,128)}) custom-call(bf16[256,384]{1,0:T(8,128)(2,1)S(1)} %get-tuple-element.10.refs_0_, bf16[256,384]{1,0:T(8,128)(2,1)S(1)} %get-tuple-element.11.refs_1_, ...), custom_call_target="tpu_custom_call" | custom-call | tf_op jit(solution)/shard_map/pallas_call | solution.py:693

commit v6 on v5

--- a/solution.py
+++ b/solution.py
@@ -72,7 +72,6 @@
 def layer_kernel(
     z_size,
     q_hbm, k_hbm, v_hbm, w_hbm, g_hbm,
-    proj_out, dq_out, dk_out, dv_out, dw_out,
     proj_ref, dq_ref, dk_ref, dv_ref, dw_ref,
     q_ref, k_ref, v_ref, w_ref, packs, q_in, do_in, k_in, v_in, att_in, dq_in, dk_in, dv_in,
     grads, grads_t, k_nat, v_nat, k_tr, v_tr, q_tr, do_tr,
@@ -80,7 +79,7 @@
     near_send, near_in, back_send, back_in, attended,
     proj_send, proj_in, proj_keep, hip_send, hip_in,
     x_terms, x_in, z_send, z_in, z_terms, z_first_in, x_send, x_last_in, y_send, y_in, sums,
-    load_sems, store_sems, a2a_send_sems, a2a_recv_sems, flow_sems, near_sems, back_sems, term_sems,
+    load_sems, a2a_send_sems, a2a_recv_sems, flow_sems, near_sems, back_sems, term_sems,
     grad_send_sems, grad_recv_sems, proj_send_sems, proj_recv_sems, x_sems, z_sems, z_first_sems, x_last_sems, y_sems,
 ):
     seq = lax.axis_index("seq")
@@ -175,13 +174,6 @@
     pl.semaphore_wait(barrier, greeted)
 
     started = []
-    stores = []
-
-    def store(src, dst):
-        copy = pltpu.make_async_copy(src, dst, store_sems.at[len(stores)])
-        copy.start()
-        stores.append(copy)
-
 
     def remote(src, dst, send_sem, recv_sem, target):
         return pltpu.make_async_remote_copy(
@@ -556,32 +548,25 @@
     for j in range(2):
         swap_wait(DQ, j, dq_in.at[j])
     from_pieces(dq_in, dq_ref)
-    store(dq_ref, dq_out)
     remote(proj_send.at[1], proj_in.at[1], proj_send_sems.at[1], proj_recv_sems.at[1], sibling).wait_recv()
     hip_copy.wait_recv()
     proj_ref[...] = (proj_keep[1] + proj_in[1].astype(F32) + hip_in[...].astype(F32)).astype(BF16)
-    store(proj_ref, proj_out)
     for j in range(2):
         swap_wait(DK, j, dk_in.at[j])
     from_pieces(dk_in, dk_ref)
-    store(dk_ref, dk_out)
     for j in range(2):
         swap_wait(DV, j, dv_in.at[j])
     from_pieces(dv_in, dv_ref)
-    store(dv_ref, dv_out)
     result = y_send[y_at]
     for step in range(1, Y_SIZE):
         y_copies[step - 1].wait_recv()
         result += y_in[step - 1]
     dw_ref[...] = result[0:out_rows]
-    store(dw_ref, dw_out)
 
     for copy in started:
         copy.wait_send()
     for sent, wait in waits:
         pl.when(sent)(wait)
-    for copy in stores:
-        copy.wait()
 
 
 def results_kernel(*refs):
@@ -606,11 +591,6 @@
     dma = pltpu.SemaphoreType.DMA
     piece = (PIECE, LANES)
     scratch = [
-        vmem((SPAN, COLS), BF16),
-        vmem((SPAN, COLS), BF16),
-        vmem((SPAN, COLS), BF16),
-        vmem((SPAN, COLS), BF16),
-        vmem((out_rows, COLS), F32),
         vmem((SPAN, COLS), BF16),
         vmem((SPAN, COLS), BF16),
         vmem((SPAN, COLS), BF16),
@@ -661,7 +641,6 @@
         vmem((Y_SIZE - 1, padded, COLS), F32),
         vmem((block, COLS), F32),
         dma((5,)),
-        dma((5,)),
         dma((8, 2)),
         dma((8, 2)),
         dma((2, 2, 2)),
@@ -684,7 +663,7 @@
         functools.partial(layer_kernel, z_size),
         out_shape=outputs,
         in_specs=[anywhere] * 5,
-        out_specs=(anywhere,) * 5,
+        out_specs=(pl.BlockSpec(memory_space=pltpu.VMEM),) * 5,
         scratch_shapes=scratch,
         compiler_params=pltpu.CompilerParams(
             collective_id=0, has_side_effects=True, vmem_limit_bytes=53 * 1024 * 1024

time: 77.7 us -> 77.6 us (level)
  no operation moved by 1% of the time
where the time goes in v6:
time: 77.6 us; the launch traced here: 76.9 us
  Pallas kernels  76.3 us (98%)
    pallas_call x1, Pallas kernels, shards(): pl.pallas_call(functools.partial(layer_kernel, z_size), out_shape=outputs...  75.4 us

profile of v6, /device:TPU:1, one launch (start us, length us, event | category | flops | bytes accessed | tf_op | source)
XLA Modules:
  0.0 76.9 jit_solution(3350465916714162620)
XLA Ops:
  0.6 75.4 %shard_map.92 = (bf16[256,384]{1,0:T(8,128)(2,1)S(1)}, bf16[256,384]{1,0:T(8,128)(2,1)S(1)}, bf16[256,384]{1,0:T(8,128)(2,1)S(1)}, bf16[256,384]{1,0:T(8,128)(2,1)S(1)}, f32[12,384]{1,0:T(8,128)S(1)}) custom-call(bf16[256,384]{1,0:T(8,128)(2,1)} %q_hbm.1, bf16[256,384]{1,0:T(8,128)(2,1)} %k_hbm.1, bf16[256,384]{1,0:T(8,128)(2,1)} %v_hbm.1, ...), custom_call_target="tpu_custom_call" | custom-call | tf_op jit(solution)/shard_map/pallas_call | solution.py:662
  76.0 0.9 %shard_map.93 = (bf16[256,384]{1,0:T(8,128)(2,1)}, bf16[256,384]{1,0:T(8,128)(2,1)}, bf16[256,384]{1,0:T(8,128)(2,1)}, bf16[256,384]{1,0:T(8,128)(2,1)}, f32[12,384]{1,0:T(8,128)}) custom-call(bf16[256,384]{1,0:T(8,128)(2,1)S(1)} %get-tuple-element.10.refs_0_, bf16[256,384]{1,0:T(8,128)(2,1)S(1)} %get-tuple-element.11.refs_1_, ...), custom_call_target="tpu_custom_call" | custom-call | tf_op jit(solution)/shard_map/pallas_call | solution.py:672

commit v7 on v6

--- a/solution.py
+++ b/solution.py
@@ -149,12 +149,6 @@
         loads[name].start()
     loads["k"].wait()
     to_pieces(tiles_of(k_ref), packs.at[K])
-    loads["v"].wait()
-    to_pieces(tiles_of(v_ref), packs.at[V])
-    loads["q"].wait()
-    to_pieces(tiles_of(q_ref), packs.at[Q], HEAD_DIM**-0.5)
-    loads["g"].wait()
-
     @pl.when(jnp.logical_not(has_before))
     def _():
         k_in[0:2] = jnp.zeros((2, PIECE, LANES), BF16)
@@ -208,9 +202,15 @@
         slot = grads.at[from_step[step]]
         remote(slot, slot, grad_send_sems.at[step - 1], grad_recv_sems.at[step - 1], across).wait_recv()
 
-    for kind, buffer in ((K, k_in), (V, v_in)):
-        for j in range(2):
-            swap_start(kind, j, packs.at[kind, j], buffer.at[4 + y_low])
+    for j in range(2):
+        swap_start(K, j, packs.at[K, j], k_in.at[4 + y_low])
+    loads["v"].wait()
+    to_pieces(tiles_of(v_ref), packs.at[V])
+    for j in range(2):
+        swap_start(V, j, packs.at[V, j], v_in.at[4 + y_low])
+    loads["q"].wait()
+    to_pieces(tiles_of(q_ref), packs.at[Q], HEAD_DIM**-0.5)
+    loads["g"].wait()
     for j in range(2):
         swap_start(Q, j, packs.at[Q, j], q_in.at[y_low])
 

time: 77.6 us -> 77.6 us (level)
  no operation moved by 1% of the time
where the time goes in v7:
time: 77.6 us; the launch traced here: 76.9 us
  Pallas kernels  76.3 us (98%)
    pallas_call x1, Pallas kernels, shards(): pl.pallas_call(functools.partial(layer_kernel, z_size), out_shape=outputs...  75.4 us

profile of v7, /device:TPU:1, one launch (start us, length us, event | category | flops | bytes accessed | tf_op | source)
XLA Modules:
  0.0 76.9 jit_solution(15695502606535206861)
XLA Ops:
  0.6 75.4 %shard_map.92 = (bf16[256,384]{1,0:T(8,128)(2,1)S(1)}, bf16[256,384]{1,0:T(8,128)(2,1)S(1)}, bf16[256,384]{1,0:T(8,128)(2,1)S(1)}, bf16[256,384]{1,0:T(8,128)(2,1)S(1)}, f32[12,384]{1,0:T(8,128)S(1)}) custom-call(bf16[256,384]{1,0:T(8,128)(2,1)} %q_hbm.1, bf16[256,384]{1,0:T(8,128)(2,1)} %k_hbm.1, bf16[256,384]{1,0:T(8,128)(2,1)} %v_hbm.1, ...), custom_call_target="tpu_custom_call" | custom-call | tf_op jit(solution)/shard_map/pallas_call | solution.py:662
  76.0 0.9 %shard_map.93 = (bf16[256,384]{1,0:T(8,128)(2,1)}, bf16[256,384]{1,0:T(8,128)(2,1)}, bf16[256,384]{1,0:T(8,128)(2,1)}, bf16[256,384]{1,0:T(8,128)(2,1)}, f32[12,384]{1,0:T(8,128)}) custom-call(bf16[256,384]{1,0:T(8,128)(2,1)S(1)} %get-tuple-element.10.refs_0_, bf16[256,384]{1,0:T(8,128)(2,1)S(1)} %get-tuple-element.11.refs_1_, ...), custom_call_target="tpu_custom_call" | custom-call | tf_op jit(solution)/shard_map/pallas_call | solution.py:672
